TPU v7x, 32 devices: a whole 2x2x4 slice. The times are simulated.
32 devices in a mesh: dp: 8 (over z, x), comp: 4 (over y, core).
Axes of the slice: x: 2, y: 2, z: 4, core: 2. Of those that a mesh axis runs over, the one named last changes fastest.
Arguments:
- climate_vector: bfloat16 [8, 4, 360, 256], P('dp', 'comp'), may hold values from -6 to 6
- pelagic_vector: bfloat16 [8, 8, 720, 128], P('dp', None, 'comp'), may hold values from -6 to 6
- wet_land_flags: int32 [8, 720], P(None, 'comp'), may hold values 0 or 1
- sky_convolution_weights: bfloat16 [9, 256, 256], replicated, may hold values from -0.125 to 0.125
- pelagic_convolution_weights: bfloat16 [9, 128, 128], replicated, may hold values from -0.1875 to 0.1875
- interface_emission_map: bfloat16 [256, 128], replicated, may hold values from -0.375 to 0.375
- thermal_drive_linear_map: bfloat16 [128, 256], replicated, may hold values from -0.5 to 0.5
- regrid_donor_ids: int32 [8, 720, 4], P('comp'), may hold values from 0 to 1439, as said below
- regrid_donor_factors: float32 [8, 720, 4], P('comp'), as said below
- thermal_donor_ids: int32 [4, 360, 4], P('comp'), may hold values from 0 to 5759, as said below
- thermal_donor_factors: float32 [4, 360, 4], P('comp'), as said below
- upcoming_sky_sensitivity: bfloat16 [8, 4, 360, 256], P('dp', 'comp'), may hold values from -6 to 6
- upcoming_pelagic_sensitivity: bfloat16 [8, 8, 720, 128], P('dp', None, 'comp'), may hold values from -6 to 6
Outputs:
- atmos_next: float32 [8, 4, 360, 256], P('dp', 'comp')
- ocean_next: float32 [8, 8, 720, 128], P('dp', None, 'comp')
- atmos_kernel_grad: float32 [9, 256, 256], P(None, 'dp', 'comp')
- ocean_kernel_grad: float32 [9, 128, 128], P(None, 'dp', 'comp')
Inputs may be any that keep to these rules, and one draw needn't show every extreme that they name: `regrid_donor_ids`: the sources of ocean cell (r, j) are atmosphere cells in the same band of 1 row as row r // 2, within one longitude of j // 2, cyclically. `regrid_donor_factors`: positive; the 4 shares of a cell sum to one. `thermal_donor_ids`: the sources of atmosphere cell (r, l) are ocean cells in rows 2r or 2r + 1 and longitudes 2l - 1 to 2l + 2, cyclically. `thermal_donor_factors`: positive; the 4 shares of a cell sum to one.
All inputs are finite; a program needn't handle non-finite values. No bound on the sum of `wet_land_flags` on one device may be relied on, other than what follows from the above.
Results may differ from a plain program's by a relative error of at most 0.004.
Values may be sent and summed in bfloat16 or wider, within the bound.
A program may use at most 64 MiB of HBM per device.

v0:
```python
import jax
import jax.numpy as jnp
from jax import lax
from jax.sharding import PartitionSpec as P


def with_halo(cells, sides, width, closed):
    for axis, dim in sides:
        count = lax.axis_size(axis)
        ends = count if closed else count - 1
        head = lax.slice_in_dim(cells, 0, width, axis=dim)
        tail = lax.slice_in_dim(cells, cells.shape[dim] - width, cells.shape[dim], axis=dim)
        cells = jnp.concatenate(
            [
                lax.ppermute(tail, axis, [(i, (i + 1) % count) for i in range(ends)]),
                cells,
                lax.ppermute(head, axis, [((i + 1) % count, i) for i in range(ends)]),
            ],
            axis=dim,
        )
    return cells


def convolve(padded, kernel):
    sample_batch = padded.shape[0]
    rows = padded.shape[1] - 2
    cols = padded.shape[2] - 2
    width = padded.shape[3]
    total = jnp.zeros((sample_batch * rows * cols, kernel.shape[2]), jnp.float32)
    for tap_row in range(3):
        for tap_col in range(3):
            window = padded[:, tap_row : tap_row + rows, tap_col : tap_col + cols].reshape(
                -1, width
            )
            total = total + jnp.dot(
                window, kernel[3 * tap_row + tap_col], preferred_element_type=jnp.float32
            )
    return total.reshape(sample_batch, rows, cols, -1)


def kernel_terms(padded, delta):
    rows = padded.shape[1] - 2
    cols = padded.shape[2] - 2
    width = padded.shape[3]
    flat_delta = delta.reshape(-1, delta.shape[-1])
    taps = []
    for tap_row in range(3):
        for tap_col in range(3):
            window = padded[:, tap_row : tap_row + rows, tap_col : tap_col + cols].reshape(
                -1, width
            )
            taps.append(
                lax.dot_general(
                    window, flat_delta, (((0,), (0,)), ((), ())), preferred_element_type=jnp.float32
                )
            )
    return jnp.stack(taps)


def silu_slope(value):
    logistic = jax.nn.sigmoid(value)
    return logistic * (1.0 + value * (1.0 - logistic))


def per_device(
    climate_vector,
    pelagic_vector,
    wet_land_flags,
    sky_convolution_weights,
    pelagic_convolution_weights,
    interface_emission_map,
    thermal_drive_linear_map,
    regrid_donor_ids,
    regrid_donor_factors,
    thermal_donor_ids,
    thermal_donor_factors,
    upcoming_sky_sensitivity,
    upcoming_pelagic_sensitivity,
):
    sample_batch, band_rows, atmos_lons, atmos_width = climate_vector.shape
    ocean_rows, band_lons, ocean_grid_width = (
        pelagic_vector.shape[1],
        pelagic_vector.shape[2],
        pelagic_vector.shape[3],
    )
    bands = lax.axis_size("comp")
    parallel_slice = lax.axis_index("comp")
    coupled_entry_pairs = 2 * band_rows
    pelagic_east_total = band_lons * bands
    near = regrid_donor_ids.shape[2]
    ocean_blocks = pelagic_vector.reshape(
        sample_batch, bands, coupled_entry_pairs, band_lons, ocean_grid_width
    )
    surface_exchange_input = lax.all_to_all(
        ocean_blocks, "comp", split_axis=1, concat_axis=1, tiled=True
    )
    flux_cells = jnp.dot(
        climate_vector.reshape(-1, atmos_width),
        interface_emission_map,
        preferred_element_type=jnp.float32,
    )
    flux_cells = flux_cells.astype(jnp.bfloat16)
    cells_flat = flux_cells.reshape(sample_batch, band_rows * atmos_lons, ocean_grid_width)
    local_flux = regrid_donor_ids - parallel_slice * (band_rows * atmos_lons)
    local_flux = local_flux.reshape(coupled_entry_pairs, bands, band_lons, near).transpose(
        1, 0, 2, 3
    )
    flux_weights = regrid_donor_factors.reshape(
        coupled_entry_pairs, bands, band_lons, near
    ).transpose(1, 0, 2, 3)
    flux_taken = jnp.take(cells_flat, local_flux, axis=1).astype(jnp.float32)
    flux_send = jnp.sum(flux_taken * flux_weights[None, ..., None], axis=4).astype(jnp.bfloat16)
    flux_in = lax.all_to_all(flux_send, "comp", split_axis=1, concat_axis=1, tiled=True)
    padded_a = with_halo(climate_vector, (("comp", 1),), 1, False)
    padded_a = jnp.concatenate([padded_a[:, :, -1:], padded_a, padded_a[:, :, :1]], axis=2)
    conv_a = convolve(padded_a, sky_convolution_weights)
    padded_o = with_halo(pelagic_vector, (("comp", 2),), 1, True)
    padded_o = jnp.pad(padded_o, ((0, 0), (1, 1), (0, 0), (0, 0)))
    conv_o = convolve(padded_o, pelagic_convolution_weights)
    source_row_index = (
        thermal_donor_ids // pelagic_east_total - parallel_slice * coupled_entry_pairs
    )
    donor_east_ids = thermal_donor_ids % pelagic_east_total
    nearby_thermal_values = (
        donor_east_ids // band_lons * coupled_entry_pairs + source_row_index
    ) * band_lons + donor_east_ids % band_lons
    pelagic_picked_sites = jnp.take(
        surface_exchange_input.reshape(sample_batch, -1, ocean_grid_width),
        nearby_thermal_values,
        axis=1,
    ).astype(jnp.float32)
    interface_coupling_terms = jnp.sum(
        pelagic_picked_sites * thermal_donor_factors[None, ..., None], axis=3
    ).astype(jnp.bfloat16)
    atmosphere_forcing = jnp.dot(
        interface_coupling_terms.reshape(-1, ocean_grid_width),
        thermal_drive_linear_map,
        preferred_element_type=jnp.float32,
    )
    za = conv_a + atmosphere_forcing.reshape(sample_batch, band_rows, atmos_lons, atmos_width)
    atmos_next = climate_vector.astype(jnp.float32) + jax.nn.silu(za)
    flux_ocean = flux_in.reshape(sample_batch, ocean_rows, band_lons, ocean_grid_width)
    wet = wet_land_flags.astype(jnp.float32)[None, :, :, None]
    zo = conv_o + flux_ocean.astype(jnp.float32)
    ocean_next = pelagic_vector.astype(jnp.float32) + wet * jax.nn.silu(zo)
    delta_a = (upcoming_sky_sensitivity.astype(jnp.float32) * silu_slope(za)).astype(jnp.bfloat16)
    delta_o = (upcoming_pelagic_sensitivity.astype(jnp.float32) * wet * silu_slope(zo)).astype(
        jnp.bfloat16
    )
    grad_a = kernel_terms(padded_a, delta_a)
    grad_o = kernel_terms(padded_o, delta_o)
    banded = (
        lax.psum_scatter(grad_a, "comp", scatter_dimension=2, tiled=True),
        lax.psum_scatter(grad_o, "comp", scatter_dimension=2, tiled=True),
    )
    summed = (
        lax.psum_scatter(banded[0], "dp", scatter_dimension=1, tiled=True),
        lax.psum_scatter(banded[1], "dp", scatter_dimension=1, tiled=True),
    )
    return (atmos_next, ocean_next, summed[0], summed[1])


def solution(mesh):
    placed = (
        P("dp", "comp", None, None),
        P("dp", None, "comp", None),
        P(None, "comp"),
        P(),
        P(),
        P(),
        P(),
        P("comp", None, None),
        P("comp", None, None),
        P("comp", None, None),
        P("comp", None, None),
        P("dp", "comp", None, None),
        P("dp", None, "comp", None),
    )
    return jax.shard_map(
        per_device,
        mesh=mesh,
        in_specs=placed,
        out_specs=(
            P("dp", "comp", None, None),
            P("dp", None, "comp", None),
            P(None, "dp", "comp"),
            P(None, "dp", "comp"),
        ),
        check_vma=False,
    )
```

profile of v0, /device:TPU:0, one launch (start us, length us, event | category | flops | bytes accessed | tf_op | source)
XLA Modules:
  0.0 307.7 jit_solution(7630401700142352803)
XLA Ops:
  7.2 3.2 %collective-permute-start = (bf16[1,1,360,256]{3,2,1,0:T(8,128)(2,1)}, bf16[1,1,360,256]{3,2,1,0:T(8,128)(2,1)}, u32[]{:S(2)}, u32[]{:S(2)}) collective-permute-start(bf16[1,1,360,256]{3,2,1,0:T(8,128)(2,1)} %param.13), channel_id=1, source_target_pairs={{0,1},{1,2},{2,3},{4,5},{5,6},{6,7},{8,9},{9,10},{10,11},{12,13},{... | collective-permute-start | bytes 552968 | tf_op jit(solution)/shard_map/ppermute | solution.py:15
  10.4 1.3 collective-permute-start.1
  12.7 2.6 collective-permute-start.2
  17.9 11.5 %gather_fusion.1 = bf16[5760,128]{1,0:T(8,128)(2,1)S(1)} fusion(bf16[360,128]{1,0:T(8,128)(2,1)S(1)} %convolution_convert_fusion, s32[6144]{0:T(1024)S(1)} %pad_clamp_fusion), kind=kCustom, calls=%fused_computation.1 | custom fusion | bytes 2972160 | tf_op jit(solution)/shard_map/jit(_take)/gather | solution.py:111
  29.4 8.5 %multiply_reduce_fusion = bf16[4,2,180,128]{3,2,1,0:T(8,128)(2,1)S(1)} fusion(f32[4,2,180,4]{3,2,1,0:T(8,128)S(1)} %copy.189, bf16[1,4,2,180,4,128]{5,4,3,2,1,0:T(4,128)(2,1)S(1)} %bitcast.287, pred[4,2,180,4]{3,2,1,0:T(8,128)(4,1)S(1)} %compare_and_fusion), kind=kLoop, calls=%fused_computation.2 | loop fusion | flops 2764800 | bytes 1872000 | tf_op jit(solution)/shard_map/reduce_sum | solution.py:112
  38.9 4.6 %all-to-all-start.1 = ((bf16[1,4,2,180,128]{4,2,3,0,1:T(2,128)(2,1)}), bf16[1,4,2,180,128]{4,2,3,0,1:T(2,128)(2,1)}, u32[]{:S(2)}, u32[]{:S(2)}) async-start(bf16[1,4,2,180,128]{4,2,3,0,1:T(2,128)(2,1)} %copy.190), calls=%async_computation.1 | async-start | bytes 737280 | tf_op jit(solution)/shard_map/all_to_all | solution.py:113
  43.9 1.9 fusion.90
  48.6 1.2 fusion.116
  50.5 1.2 fusion.95
  54.4 1.8 reshape.319
  56.2 2.1 fusion.87
  60.7 1.3 convolution_add_fusion.5
  62.0 1.3 convolution_add_fusion.4
  63.3 1.4 fusion.1
  66.9 1.9 convolution_add_fusion
  68.8 1.2 reshape.322
  72.0 1.4 fusion.63
  76.0 4.1 %all-to-all-start = ((bf16[1,4,2,180,128]{4,2,3,0,1:T(2,128)(2,1)}), bf16[1,4,2,180,128]{4,2,3,0,1:T(2,128)(2,1)}, u32[]{:S(2)}, u32[]{:S(2)}) async-start(bf16[1,4,2,180,128]{4,2,3,0,1:T(2,128)(2,1)} %copy.177), calls=%async_computation | async-start | bytes 737280 | tf_op jit(solution)/shard_map/all_to_all | solution.py:94
  81.3 1.4 multiply_convert_fusion
  85.6 1.4 copy.201
  88.5 3.4 %gather_fusion = bf16[1440,128]{1,0:T(8,128)(2,1)S(1)} fusion(bf16[1440,128]{1,0:T(8,128)(2,1)S(1)} %reshape.338, s32[2048]{0:T(1024)S(1)} %pad_clamp_fusion.1), kind=kCustom, calls=%fused_computation | custom fusion | bytes 743040 | tf_op jit(solution)/shard_map/jit(_take)/gather | solution.py:127
  91.9 2.1 multiply_reduce_fusion.1
  96.1 1.9 fusion.10
  104.9 5.0 %copy.196 = f32[9,256,256]{1,0,2:T(8,128)} copy(f32[9,256,256]{2,1,0:T(8,128)} %fusion.3) | data formatting | bytes 4718592 | tf_op jit(solution)/shard_map/stack | solution.py:57
  110.0 4.6 %reduce-scatter.9.cloned.1.call-done = f32[9,128,32]{1,0,2:T(8,128)} async-done(((f32[9,128,128]{1,0,2:T(8,128)}), f32[9,128,32]{1,0,2:T(8,128)}) %reduce-scatter.9.cloned.1.call-update) | async-done | bytes 147472 | tf_op jit(solution)/shard_map/reduce_scatter | solution.py:154
  114.6 2.4 copy.202
  117.1 44.8 %reduce-scatter.5.cloned.1.call-done = f32[9,256,64]{1,0,2:T(8,128)} async-done(((f32[9,256,256]{1,0,2:T(8,128)}), f32[9,256,64]{1,0,2:T(8,128)}) %reduce-scatter.5.cloned.1.call-update) | async-done | bytes 589840 | tf_op jit(solution)/shard_map/reduce_scatter | solution.py:153
  161.9 3.9 %copy.197 = f32[9,256,64]{2,0,1:T(8,128)} copy(f32[9,256,64]{1,0,2:T(8,128)} %reduce-scatter.5.cloned.1.call-done) | data formatting | bytes 1179648 | tf_op jit(solution)/shard_map/reduce_scatter | solution.py:153
  166.8 62.0 %reduce-scatter.11.cloned.1.call-done = f32[9,16,32]{2,0,1:T(8,128)} async-done(((f32[9,128,32]{2,0,1:T(8,128)}), f32[9,16,32]{2,0,1:T(8,128)}) %reduce-scatter.11.cloned.1.call-update) | async-done | bytes 18448 | tf_op jit(solution)/shard_map/reduce_scatter | solution.py:158
  228.8 1.6 copy.205
  230.4 69.1 %reduce-scatter.7.cloned.1.call-done = f32[9,32,64]{2,0,1:T(8,128)} async-done(((f32[9,256,64]{2,0,1:T(8,128)}), f32[9,32,64]{2,0,1:T(8,128)}) %reduce-scatter.7.cloned.1.call-update) | async-done | bytes 73744 | tf_op jit(solution)/shard_map/reduce_scatter | solution.py:157
  299.5 1.7 copy.204
  (148 shorter events, 35.6 us)
Async XLA Ops:
  7.2 86.8 %copy-start = (bf16[128,256]{1,0:T(8,128)(2,1)S(1)}, bf16[128,256]{1,0:T(8,128)(2,1)}, u32[]{:S(2)}) copy-start(bf16[128,256]{1,0:T(8,128)(2,1)} %param.19) | copy-start | bytes 196612
  7.2 10.1 %copy-start.3 = (bf16[1,1,360,256]{3,2,1,0:T(8,128)(2,1)S(1)}, bf16[1,1,360,256]{3,2,1,0:T(8,128)(2,1)}, u32[]{:S(2)}) copy-start(bf16[1,1,360,256]{3,2,1,0:T(8,128)(2,1)} %param.13) | copy-start | bytes 552964
  7.2 10.1 %copy-start.26 = (bf16[256,128]{1,0:T(8,128)(2,1)S(1)}, bf16[256,128]{1,0:T(8,128)(2,1)}, u32[]{:S(2)}) copy-start(bf16[256,128]{1,0:T(8,128)(2,1)} %param.18) | copy-start | bytes 196612
  7.2 62.8 %collective-permute-start = (bf16[1,1,360,256]{3,2,1,0:T(8,128)(2,1)}, bf16[1,1,360,256]{3,2,1,0:T(8,128)(2,1)}, u32[]{:S(2)}, u32[]{:S(2)}) collective-permute-start(bf16[1,1,360,256]{3,2,1,0:T(8,128)(2,1)} %param.13), channel_id=1, source_target_pairs={{0,1},{1,2},{2,3},{4,5},{5,6},{6,7},{8,9},{9,10},{10,11},{12,13},{... | collective-permute-start | bytes 552968 | tf_op jit(solution)/shard_map/ppermute | solution.py:15
  10.4 60.7 %collective-permute-start.1 = (bf16[1,1,360,256]{3,2,1,0:T(8,128)(2,1)}, bf16[1,1,360,256]{3,2,1,0:T(8,128)(2,1)S(1)}, u32[]{:S(2)}, u32[]{:S(2)}) collective-permute-start(bf16[1,1,360,256]{3,2,1,0:T(8,128)(2,1)} %param.13), channel_id=1, source_target_pairs={{1,0},{2,1},{3,2},{5,4},{6,5},{7,6},{9,8},{10,9},{11,10},{13,12},{... | collective-permute-start | bytes 552968 | tf_op jit(solution)/shard_map/ppermute | solution.py:17
  12.7 4.8 %copy-start.27 = (f32[2,720,4]{1,2,0:T(4,128)S(1)}, f32[2,720,4]{1,2,0:T(4,128)}, u32[]{:S(2)}) copy-start(f32[2,720,4]{1,2,0:T(4,128)} %param.21) | copy-start | bytes 69124
  12.7 35.7 %collective-permute-start.2 = (bf16[1,8,1,128]{3,2,1,0:T(2,128)(2,1)S(1)}, bf16[1,8,1,128]{3,2,1,0:T(2,128)(2,1)S(1)}, u32[]{:S(2)}, u32[]{:S(2)}) collective-permute-start(bf16[1,8,1,128]{3,2,1,0:T(2,128)(2,1)S(1)} %get-tuple-element.51), channel_id=1, source_target_pairs={{0,1},{1,2},{2,3},{3,0},{4,5},{5,6},{6,7},{7,4},{8,9},{9,10},{10,1... | collective-permute-start | bytes 6152 | tf_op jit(solution)/shard_map/ppermute | solution.py:15
  15.4 33.1 %collective-permute-start.3 = (bf16[1,8,1,128]{3,2,1,0:T(2,128)(2,1)S(1)}, bf16[1,8,1,128]{3,2,1,0:T(2,128)(2,1)S(1)}, u32[]{:S(2)}, u32[]{:S(2)}) collective-permute-start(bf16[1,8,1,128]{3,2,1,0:T(2,128)(2,1)S(1)} %get-tuple-element.52), channel_id=1, source_target_pairs={{1,0},{2,1},{3,2},{0,3},{5,4},{6,5},{7,6},{4,7},{9,8},{10,9},{11,1... | collective-permute-start | bytes 6152 | tf_op jit(solution)/shard_map/ppermute | solution.py:17
  29.4 14.2 %copy-start.30 = (s32[1,360,4]{1,2,0:T(4,128)S(1)}, s32[1,360,4]{1,2,0:T(4,128)}, u32[]{:S(2)}) copy-start(s32[1,360,4]{1,2,0:T(4,128)} %param.22) | copy-start | bytes 17284
  37.9 7.9 %copy-start.28 = (s32[8,180]{1,0:T(8,128)S(1)}, s32[8,180]{1,0:T(8,128)}, u32[]{:S(2)}) copy-start(s32[8,180]{1,0:T(8,128)} %param.15) | copy-start | bytes 17284
  37.9 7.9 %copy-start.1 = (bf16[1,8,180,128]{3,1,2,0:T(8,128)(2,1)S(1)}, bf16[1,8,180,128]{3,1,2,0:T(8,128)(2,1)}, u32[]{:S(2)}) copy-start(bf16[1,8,180,128]{3,1,2,0:T(8,128)(2,1)} %param.14) | copy-start | bytes 1105924
  37.9 9.7 %copy-start.29 = (f32[1,360,4]{1,2,0:T(4,128)S(1)}, f32[1,360,4]{1,2,0:T(4,128)}, u32[]{:S(2)}) copy-start(f32[1,360,4]{1,2,0:T(4,128)} %param.23) | copy-start | bytes 17284
  38.9 37.0 %all-to-all-start.1 = ((bf16[1,4,2,180,128]{4,2,3,0,1:T(2,128)(2,1)}), bf16[1,4,2,180,128]{4,2,3,0,1:T(2,128)(2,1)}, u32[]{:S(2)}, u32[]{:S(2)}) async-start(bf16[1,4,2,180,128]{4,2,3,0,1:T(2,128)(2,1)} %copy.190), calls=%async_computation.1 | async-start | bytes 737280 | tf_op jit(solution)/shard_map/all_to_all | solution.py:113
  53.6 5.5 %copy-start.17 = (bf16[1,8,180,128]{3,2,1,0:T(8,128)(2,1)S(1)}, bf16[1,8,180,128]{3,2,1,0:T(8,128)(2,1)}, u32[]{:S(2)}) copy-start(bf16[1,8,180,128]{3,2,1,0:T(8,128)(2,1)} %get-tuple-element.44) | copy-start | bytes 1105924
  60.7 2.6 copy-start.18
  62.0 2.8 copy-start.2
  62.0 2.8 copy-start.19
  76.0 11.4 %all-to-all-start = ((bf16[1,4,2,180,128]{4,2,3,0,1:T(2,128)(2,1)}), bf16[1,4,2,180,128]{4,2,3,0,1:T(2,128)(2,1)}, u32[]{:S(2)}, u32[]{:S(2)}) async-start(bf16[1,4,2,180,128]{4,2,3,0,1:T(2,128)(2,1)} %copy.177), calls=%async_computation | async-start | bytes 737280 | tf_op jit(solution)/shard_map/all_to_all | solution.py:94
  80.1 34.6 %reduce-scatter.9.cloned.1.call-start = ((), (), s32[]{:S(2)}) async-start(), calls=%async_computation.8 | async-start | bytes 1310720 | tf_op jit(solution)/shard_map/reduce_scatter | solution.py:154
  87.1 4.8 %copy-start.23 = (f32[360,4]{1,0:T(8,128)S(1)}, f32[360,4]{1,0:T(8,128)}, u32[]{:S(2)}) copy-start(f32[360,4]{1,0:T(8,128)} %copy.180) | copy-start | bytes 17284
  87.1 4.8 %copy-start.25 = (pred[360,4]{1,0:T(8,128)(4,1)S(1)}, pred[360,4]{1,0:T(8,128)(4,1)}, u32[]{:S(2)}) copy-start(pred[360,4]{1,0:T(8,128)(4,1)} %copy.175) | copy-start | bytes 4324
  87.1 74.8 %reduce-scatter.5.cloned.1.call-start = ((), (), s32[]{:S(2)}) async-start(), calls=%async_computation.6 | async-start | bytes 5242880 | tf_op jit(solution)/shard_map/reduce_scatter | solution.py:153
  88.4 5.6 %copy-start.24 = (f32[360,256]{1,0:T(8,128)S(1)}, f32[360,256]{1,0:T(8,128)}, u32[]{:S(2)}) copy-start(f32[360,256]{1,0:T(8,128)} %fusion.2) | copy-start | bytes 1105924
  88.4 5.6 %copy-start.31 = (bf16[1,1,360,256]{3,2,1,0:T(8,128)(2,1)S(1)}, bf16[1,1,360,256]{3,2,1,0:T(8,128)(2,1)}, u32[]{:S(2)}) copy-start(bf16[1,1,360,256]{3,2,1,0:T(8,128)(2,1)} %param.24) | copy-start | bytes 552964
  91.9 3.2 %copy-start.13 = (bf16[360,256]{1,0:T(8,128)(2,1)S(1)}, bf16[360,256]{1,0:T(8,128)(2,1)}, u32[]{:S(2)}) copy-start(bf16[360,256]{1,0:T(8,128)(2,1)} %copy-done.12) | copy-start | bytes 552964
  91.9 6.1 %copy-start.11 = (bf16[360,256]{1,0:T(8,128)(2,1)S(1)}, bf16[360,256]{1,0:T(8,128)(2,1)}, u32[]{:S(2)}) copy-start(bf16[360,256]{1,0:T(8,128)(2,1)} %copy-done.10) | copy-start | bytes 552964
  94.0 5.0 %copy-start.9 = (bf16[360,256]{1,0:T(8,128)(2,1)S(1)}, bf16[360,256]{1,0:T(8,128)(2,1)}, u32[]{:S(2)}) copy-start(bf16[360,256]{1,0:T(8,128)(2,1)} %copy-done.8) | copy-start | bytes 552964
  94.0 7.0 %copy-start.7 = (bf16[360,256]{1,0:T(8,128)(2,1)S(1)}, bf16[360,256]{1,0:T(8,128)(2,1)}, u32[]{:S(2)}) copy-start(bf16[360,256]{1,0:T(8,128)(2,1)} %copy-done.6) | copy-start | bytes 552964
  95.1 6.9 %copy-start.5 = (bf16[360,256]{1,0:T(8,128)(2,1)S(1)}, bf16[360,256]{1,0:T(8,128)(2,1)}, u32[]{:S(2)}) copy-start(bf16[360,256]{1,0:T(8,128)(2,1)} %copy-done.4) | copy-start | bytes 552964
  95.1 7.8 %copy-start.16 = (bf16[1,1,360,256]{3,2,1,0:T(8,128)(2,1)S(1)}, bf16[1,1,360,256]{3,2,1,0:T(8,128)(2,1)}, u32[]{:S(2)}) copy-start(bf16[1,1,360,256]{3,2,1,0:T(8,128)(2,1)} %copy-done.14) | copy-start | bytes 552964
  110.0 118.9 %reduce-scatter.11.cloned.1.call-start = ((), (), s32[]{:S(2)}) async-start(), calls=%async_computation.9 | async-start | bytes 1179648 | tf_op jit(solution)/shard_map/reduce_scatter | solution.py:158
  117.0 182.5 %reduce-scatter.7.cloned.1.call-start = ((), (), s32[]{:S(2)}) async-start(), calls=%async_computation.7 | async-start | bytes 2359296 | tf_op jit(solution)/shard_map/reduce_scatter | solution.py:157
  (10 other events, 20.3 us)
Sparse Core Ops, SparseCore 0:
  87.2 27.4 reduce-scatter.8
  117.3 44.5 reduce-scatter.4
  165.3 63.4 reduce-scatter.10
  232.6 66.8 reduce-scatter.6
where the time goes:
time: 309 us; the launch traced here: 308 us
  waiting for transfers between devices  181 us (59%)
  local copies, waits for them, and re-layouts  50.7 us (16%)
  matrix products  30.8 us (10%)
  starting transfers between devices  16.2 us (5%)
  other arithmetic  14.8 us (5%)
  between operations  14.6 us (5%)
    reduce_scatter x1, waiting for transfers between devices, per_device(): lax.psum_scatter(banded[0], 'dp', scatter_dimension=1, tiled=True)  69.1 us
    reduce_scatter x1, waiting for transfers between devices, per_device(): lax.psum_scatter(banded[1], 'dp', scatter_dimension=1, tiled=True)  62 us
    reduce_scatter x1, waiting for transfers between devices, per_device(): lax.psum_scatter(grad_a, 'comp', scatter_dimension=2, tiled=True)  44.8 us
    dot_general x18, matrix products, convolve(): jnp.dot(window, kernel[3 * tap_row + tap_col], preferred_element_type=jnp...  17 us
    dot_general x18, matrix products, kernel_terms(): lax.dot_general(window, flat_delta, (((0,), (0,)), ((), ())), preferred_e...  12.6 us
    gather x1, local copies, waits for them, and re-layouts, per_device(): flux_taken = jnp.take(cells_flat, local_flux, axis=1).astype(jnp.float32)  11.5 us
    reduce_sum x1, other arithmetic, per_device(): jnp.sum(flux_taken * flux_weights[None, ..., None], axis=4)  8.5 us
    reshape x9, local copies, waits for them, and re-layouts, convolve(): padded[:, tap_row:tap_row + rows, tap_col:tap_col + cols].reshape(-1, width)  7.51 us
  transfers between devices with their start and end apart: 10, of which 4 were waited for; matrix products, arithmetic and copies ran while one was open for 31% of the time, Pallas kernels for 0%

commit v1 on v0

--- a/solution.py
+++ b/solution.py
@@ -1,6 +1,10 @@
+import functools
+
 import jax
 import jax.numpy as jnp
 from jax import lax
+from jax.experimental import pallas as pl
+from jax.experimental.pallas import tpu as pltpu
 from jax.sharding import PartitionSpec as P
 
 
@@ -38,23 +42,175 @@
     return total.reshape(sample_batch, rows, cols, -1)
 
 
-def kernel_terms(padded, delta):
+MESH = pl.DeviceIdType.MESH
+
+
+def joined_terms(padded, delta):
     rows = padded.shape[1] - 2
     cols = padded.shape[2] - 2
-    width = padded.shape[3]
     flat_delta = delta.reshape(-1, delta.shape[-1])
-    taps = []
-    for tap_row in range(3):
-        for tap_col in range(3):
-            window = padded[:, tap_row : tap_row + rows, tap_col : tap_col + cols].reshape(
-                -1, width
+    joined = jnp.concatenate([padded[:, :, b : b + cols] for b in range(3)], axis=-1)
+    return jnp.stack(
+        [
+            lax.dot_general(
+                flat_delta,
+                joined[:, a : a + rows].reshape(-1, joined.shape[-1]),
+                (((0,), (0,)), ((), ())),
+                preferred_element_type=jnp.float32,
             )
-            taps.append(
-                lax.dot_general(
-                    window, flat_delta, (((0,), (0,)), ((), ())), preferred_element_type=jnp.float32
-                )
+            for a in range(3)
+        ]
+    )
+
+
+def remote(src, dst, sems, index, target):
+    return pltpu.make_async_remote_copy(
+        src_ref=src,
+        dst_ref=dst,
+        send_sem=sems.at[0, index],
+        recv_sem=sems.at[1, index],
+        device_id=target,
+        device_id_type=MESH,
+    )
+
+
+def reduce_kernel(
+    samples, ga_ref, go_ref, outa_ref, outo_ref, r1a, r1o, s2a, s2o, r2a, r2o, da, r4, sems
+):
+    comp = lax.axis_index("comp")
+    dp = lax.axis_index("dp")
+    core = lax.rem(comp, 2)
+    half = comp // 2
+    twin = {"comp": 2 * half + 1 - core}
+    across = {"comp": 2 * (1 - half) + core}
+    barrier = pltpu.get_barrier_semaphore()
+    pl.semaphore_signal(barrier, inc=1, device_id=twin, device_id_type=MESH)
+    pl.semaphore_signal(barrier, inc=1, device_id=across, device_id_type=MESH)
+    for k in range(1, samples):
+        pl.semaphore_signal(
+            barrier, inc=1, device_id={"dp": lax.rem(dp + k, samples)}, device_id_type=MESH
+        )
+    pl.semaphore_wait(barrier, samples + 1)
+    wa = s2a.shape[1]
+    wo = s2o.shape[1]
+
+    def block(ref, width, band):
+        return ref.at[:, pl.ds(pl.multiple_of(band * width, width), width), :]
+
+    first = []
+    for n, side in enumerate((1 - half, half)):
+        band = 2 * side + 1 - core
+        first.append(
+            (
+                remote(block(ga_ref, wa, band), r1a.at[n], sems, 2 * n, twin),
+                remote(block(go_ref, wo, band), r1o.at[n], sems, 2 * n + 1, twin),
             )
-    return jnp.stack(taps)
+        )
+    for pair in first:
+        for copy in pair:
+            copy.start()
+    other = 2 * (1 - half) + core
+    first[0][0].wait_recv()
+    s2a[...] = (
+        block(ga_ref, wa, other)[...].astype(jnp.float32) + r1a[0].astype(jnp.float32)
+    ).astype(jnp.bfloat16)
+    second_a = remote(s2a, r2a, sems, 4, across)
+    second_a.start()
+    first[0][1].wait_recv()
+    s2o[...] = (
+        block(go_ref, wo, other)[...].astype(jnp.float32) + r1o[0].astype(jnp.float32)
+    ).astype(jnp.bfloat16)
+    second_o = remote(s2o, r2o, sems, 5, across)
+    second_o.start()
+    first[1][0].wait_recv()
+    first[1][1].wait_recv()
+    own_a = block(ga_ref, wa, comp)[...].astype(jnp.float32) + r1a[1].astype(jnp.float32)
+    own_o = block(go_ref, wo, comp)[...].astype(jnp.float32) + r1o[1].astype(jnp.float32)
+    second_a.wait_recv()
+    own_a = own_a + r2a[...].astype(jnp.float32)
+    second_o.wait_recv()
+    own_o = own_o + r2o[...].astype(jnp.float32)
+    ca = outa_ref.shape[1]
+    co = outo_ref.shape[1]
+    ta = own_a.reshape(3 * wa, -1)
+    ta = jnp.concatenate([ta, jnp.zeros((wa, ta.shape[1]), jnp.float32)], axis=0).T
+    to = own_o.reshape(3 * wo, -1)
+    to = jnp.concatenate([to, jnp.zeros((wo, to.shape[1]), jnp.float32)], axis=0).T
+    ta = ta.astype(jnp.bfloat16)
+    to = to.astype(jnp.bfloat16)
+    for d in range(samples):
+        for b in range(3):
+            piece = ta[(b * samples + d) * ca : (b * samples + d + 1) * ca]
+            da[d, b * ca : (b + 1) * ca, :] = piece[:, :128]
+            da[d, (3 + b) * ca : (4 + b) * ca, :] = piece[:, 128:]
+            da[d, 6 * ca + b * co : 6 * ca + (b + 1) * co, :] = to[
+                (b * samples + d) * co : (b * samples + d + 1) * co
+            ]
+    third = []
+    for k in range(1, samples):
+        peer = lax.rem(dp + k, samples)
+        copy = remote(da.at[peer], r4.at[k - 1], sems, 5 + k, {"dp": peer})
+        copy.start()
+        third.append(copy)
+    total = da[dp].astype(jnp.float32)
+    for copy, k in zip(third, range(samples)):
+        copy.wait_recv()
+        total = total + r4[k].astype(jnp.float32)
+    for a in range(3):
+        for b in range(3):
+            row = b * ca + (a // 2) * 3 * ca
+            outa_ref[3 * a + b] = total[row : row + ca, (a % 2) * wa : (a % 2 + 1) * wa]
+            row = 6 * ca + b * co
+            outo_ref[3 * a + b] = total[row : row + co, a * wo : (a + 1) * wo]
+    for pair in first:
+        for copy in pair:
+            copy.wait_send()
+    second_a.wait_send()
+    second_o.wait_send()
+    for copy in third:
+        copy.wait_send()
+
+
+def plain_sum(joined):
+    width = joined.shape[2] // 3
+    terms = joined.reshape(3, -1, 3, width).transpose(0, 2, 3, 1).reshape(9, width, -1)
+    banded = lax.psum_scatter(terms, "comp", scatter_dimension=2, tiled=True)
+    return lax.psum_scatter(banded, "dp", scatter_dimension=1, tiled=True)
+
+
+def summed_terms(ga, go):
+    samples = lax.axis_size("dp")
+    bands = lax.axis_size("comp")
+    wa, wo = ga.shape[1] // bands, go.shape[1] // bands
+    ca, co = ga.shape[2] // 3 // samples, go.shape[2] // 3 // samples
+    if bands != 4 or wa != 64 or wo != 32 or ca % 16 or co % 16:
+        return plain_sum(ga), plain_sum(go)
+    la, lo = ga.shape[2], go.shape[2]
+    piece = 6 * ca + 3 * co
+    vmem = pl.BlockSpec(memory_space=pltpu.VMEM)
+    return pl.pallas_call(
+        functools.partial(reduce_kernel, samples),
+        out_shape=(
+            jax.ShapeDtypeStruct((9, ca, wa), jnp.float32),
+            jax.ShapeDtypeStruct((9, co, wo), jnp.float32),
+        ),
+        in_specs=[vmem] * 2,
+        out_specs=(vmem, vmem),
+        scratch_shapes=[
+            pltpu.VMEM((2, 3, wa, la), jnp.bfloat16),
+            pltpu.VMEM((2, 3, wo, lo), jnp.bfloat16),
+            pltpu.VMEM((3, wa, la), jnp.bfloat16),
+            pltpu.VMEM((3, wo, lo), jnp.bfloat16),
+            pltpu.VMEM((3, wa, la), jnp.bfloat16),
+            pltpu.VMEM((3, wo, lo), jnp.bfloat16),
+            pltpu.VMEM((samples, piece, 128), jnp.bfloat16),
+            pltpu.VMEM((samples - 1, piece, 128), jnp.bfloat16),
+            pltpu.SemaphoreType.DMA((2, 5 + samples)),
+        ],
+        compiler_params=pltpu.CompilerParams(
+            collective_id=0, has_side_effects=True, vmem_limit_bytes=32 * 1024 * 1024
+        ),
+    )(ga.astype(jnp.bfloat16), go.astype(jnp.bfloat16))
 
 
 def silu_slope(value):
@@ -147,16 +303,7 @@
     delta_o = (upcoming_pelagic_sensitivity.astype(jnp.float32) * wet * silu_slope(zo)).astype(
         jnp.bfloat16
     )
-    grad_a = kernel_terms(padded_a, delta_a)
-    grad_o = kernel_terms(padded_o, delta_o)
-    banded = (
-        lax.psum_scatter(grad_a, "comp", scatter_dimension=2, tiled=True),
-        lax.psum_scatter(grad_o, "comp", scatter_dimension=2, tiled=True),
-    )
-    summed = (
-        lax.psum_scatter(banded[0], "dp", scatter_dimension=1, tiled=True),
-        lax.psum_scatter(banded[1], "dp", scatter_dimension=1, tiled=True),
-    )
+    summed = summed_terms(joined_terms(padded_a, delta_a), joined_terms(padded_o, delta_o))
     return (atmos_next, ocean_next, summed[0], summed[1])
 
 

time: 309 us -> 121 us (0.39)
  waiting for transfers between devices: 181 us -> 1.43 us
  Pallas kernels: 0 us -> 24.5 us
  matrix products: 30.8 us -> 14.3 us
  between operations: 14.6 us -> 1.31 us
  local copies, waits for them, and re-layouts: 50.7 us -> 45.4 us
    reduce_scatter x4 -> x0, waiting for transfers between devices: 181 us -> none  [the longest x1 69.1 us: per_device(): lax.psum_scatter(banded[0], 'dp', scatter_dimension=1, tiled=True)]
    pallas_call x0 -> x1, Pallas kernels: none -> 24.5 us  [summed_terms(): pl.pallas_call(functools.partial(reduce_kernel, samples), out_shape=(jax....]
    dot_general x18, matrix products: 17 us -> 8.68 us  [convolve(): jnp.dot(window, kernel[3 * tap_row + tap_col], preferred_element_type=jnp...]
    dot_general x18 -> x6, matrix products: 12.6 us -> 4.33 us  [joined_terms(): lax.dot_general(flat_delta, joined[:, a:a + rows].reshape(-1, joined.shap...]
    another operation x2 -> x0, local copies, waits for them, and re-layouts: 6.42 us -> none  [kernel_terms(): return jnp.stack(taps)]
    reduce_scatter x2 -> x0, local copies, waits for them, and re-layouts: 6.31 us -> none  [the longest x1 3.94 us: per_device(): lax.psum_scatter(grad_a, 'comp', scatter_dimension=2, tiled=True)]
    reshape x9, local copies, waits for them, and re-layouts: 7.51 us -> 12.2 us  [convolve(): padded[:, tap_row:tap_row + rows, tap_col:tap_col + cols].reshape(-1, width)]
    unnamed x70 -> x62, local copies, waits for them, and re-layouts: 7.09 us -> 6.29 us
  transfers between devices with their start and end apart: 10 -> 6, of which waited for: 4 -> 1; matrix products, arithmetic and copies ran while one was open for 31% -> 52% of each run, Pallas kernels for 0% -> 0%
where the time goes in v1:
time: 121 us; the launch traced here: 119 us
  local copies, waits for them, and re-layouts  45.4 us (38%)
  Pallas kernels  24.5 us (20%)
  starting transfers between devices  16.4 us (14%)
  other arithmetic  15.8 us (13%)
  matrix products  14.3 us (12%)
  waiting for transfers between devices  1.43 us (1%)
  between operations  1.31 us (1%)
    pallas_call x1, Pallas kernels, summed_terms(): pl.pallas_call(functools.partial(reduce_kernel, samples), out_shape=(jax....  24.5 us
    reshape x9, local copies, waits for them, and re-layouts, convolve(): padded[:, tap_row:tap_row + rows, tap_col:tap_col + cols].reshape(-1, width)  12.2 us
    gather x1, local copies, waits for them, and re-layouts, per_device(): flux_taken = jnp.take(cells_flat, local_flux, axis=1).astype(jnp.float32)  11.5 us
    dot_general x18, matrix products, convolve(): jnp.dot(window, kernel[3 * tap_row + tap_col], preferred_element_type=jnp...  8.68 us
    reduce_sum x1, other arithmetic, per_device(): jnp.sum(flux_taken * flux_weights[None, ..., None], axis=4)  8.5 us
    unnamed x62, local copies, waits for them, and re-layouts  6.29 us
    ppermute x2, starting transfers between devices, with_halo(): lax.ppermute(tail, axis, [(i, (i + 1) % count) for i in range(ends)])  5.83 us
    dot_general x6, matrix products, joined_terms(): lax.dot_general(flat_delta, joined[:, a:a + rows].reshape(-1, joined.shap...  4.33 us
  transfers between devices with their start and end apart: 6, of which 1 were waited for; matrix products, arithmetic and copies ran while one was open for 52% of the time, Pallas kernels for 0%

profile of v1, /device:TPU:0, one launch (start us, length us, event | category | flops | bytes accessed | tf_op | source)
XLA Modules:
  0.0 119.0 jit_solution(17680772193365390820)
XLA Ops:
  0.6 3.2 %collective-permute-start = (bf16[1,1,360,256]{3,2,1,0:T(8,128)(2,1)}, bf16[1,1,360,256]{3,2,1,0:T(8,128)(2,1)}, u32[]{:S(2)}, u32[]{:S(2)}) collective-permute-start(bf16[1,1,360,256]{3,2,1,0:T(8,128)(2,1)} %param.13), channel_id=1, source_target_pairs={{0,1},{1,2},{2,3},{4,5},{5,6},{6,7},{8,9},{9,10},{10,11},{12,13},{... | collective-permute-start | bytes 552968 | tf_op jit(solution)/shard_map/ppermute | solution.py:19
  3.8 1.3 %collective-permute-start.1 = (bf16[1,1,360,256]{3,2,1,0:T(8,128)(2,1)}, bf16[1,1,360,256]{3,2,1,0:T(8,128)(2,1)}, u32[]{:S(2)}, u32[]{:S(2)}) collective-permute-start(bf16[1,1,360,256]{3,2,1,0:T(8,128)(2,1)} %param.13), channel_id=1, source_target_pairs={{1,0},{2,1},{3,2},{5,4},{6,5},{7,6},{9,8},{10,9},{11,10},{13,12},{... | collective-permute-start | bytes 552968 | tf_op jit(solution)/shard_map/ppermute | solution.py:21
  5.1 1.0 copy.135
  6.2 2.6 %collective-permute-start.2 = (bf16[1,8,1,128]{3,2,1,0:T(2,128)(2,1)S(1)}, bf16[1,8,1,128]{3,2,1,0:T(2,128)(2,1)S(1)}, u32[]{:S(2)}, u32[]{:S(2)}) collective-permute-start(bf16[1,8,1,128]{3,2,1,0:T(2,128)(2,1)S(1)} %get-tuple-element.47), channel_id=1, source_target_pairs={{0,1},{1,2},{2,3},{3,0},{4,5},{5,6},{6,7},{7,4},{8,9},{9,10},{10,1... | collective-permute-start | bytes 6152 | tf_op jit(solution)/shard_map/ppermute | solution.py:19
  12.2 11.5 %gather_fusion.1 = bf16[5760,128]{1,0:T(8,128)(2,1)S(1)} fusion(bf16[360,128]{1,0:T(8,128)(2,1)S(1)} %convolution_convert_fusion.3, s32[6144]{0:T(1024)S(1)} %pad_clamp_fusion), kind=kCustom, calls=%fused_computation.1 | custom fusion | bytes 2972160 | tf_op jit(solution)/shard_map/jit(_take)/gather | solution.py:267
  23.7 8.5 %multiply_reduce_fusion = bf16[4,2,180,128]{3,2,1,0:T(8,128)(2,1)S(1)} fusion(f32[4,2,180,4]{3,2,1,0:T(8,128)S(1)} %copy.145, bf16[1,4,2,180,4,128]{5,4,3,2,1,0:T(4,128)(2,1)S(1)} %bitcast.191, pred[4,2,180,4]{3,2,1,0:T(8,128)(4,1)S(1)} %compare_and_fusion), kind=kLoop, calls=%fused_computation.2 | loop fusion | flops 2764800 | bytes 1872000 | tf_op jit(solution)/shard_map/reduce_sum | solution.py:268
  32.3 1.0 copy.146
  33.3 4.2 %all-to-all-start.1 = ((bf16[1,4,2,180,128]{4,2,3,0,1:T(2,128)(2,1)}), bf16[1,4,2,180,128]{4,2,3,0,1:T(2,128)(2,1)}, u32[]{:S(2)}, u32[]{:S(2)}) async-start(bf16[1,4,2,180,128]{4,2,3,0,1:T(2,128)(2,1)} %copy.146), calls=%async_computation.1 | async-start | bytes 737280 | tf_op jit(solution)/shard_map/all_to_all | solution.py:269
  41.5 1.2 fusion.98
  42.9 1.8 %reshape.283 = bf16[1440,128]{1,0:T(8,128)(2,1)} reshape(bf16[1,8,180,128]{3,2,1,0:T(8,128)(2,1)} %get-tuple-element.46) | data formatting | bytes 737280 | tf_op jit(solution)/shard_map/reshape | solution.py:36
  44.7 1.8 %reshape.284 = bf16[1440,128]{1,0:T(8,128)(2,1)} reshape(bf16[1,8,180,128]{3,2,1,0:T(8,128)(2,1)} %get-tuple-element.45) | data formatting | bytes 737280 | tf_op jit(solution)/shard_map/reshape | solution.py:36
  46.5 1.8 %reshape.285 = bf16[1440,128]{1,0:T(8,128)(2,1)} reshape(bf16[1,8,180,128]{3,2,1,0:T(8,128)(2,1)} %get-tuple-element.44) | data formatting | bytes 737280 | tf_op jit(solution)/shard_map/reshape | solution.py:36
  49.9 1.8 %reshape.286 = bf16[1440,128]{1,0:T(8,128)(2,1)} reshape(bf16[1,8,180,128]{3,2,1,0:T(8,128)(2,1)} %copy.140) | data formatting | bytes 737280 | tf_op jit(solution)/shard_map/reshape | solution.py:36
  51.7 1.8 %copy.143 = bf16[1,8,180,128]{3,2,1,0:T(8,128)(2,1)} copy(bf16[1,8,180,128]{3,1,2,0:T(8,128)(2,1)} %get-tuple-element.51) | data formatting | bytes 737280 | tf_op jit(solution)/shard_map/slice | solution.py:36
  53.5 1.8 %reshape.288 = bf16[1440,128]{1,0:T(8,128)(2,1)} reshape(bf16[1,8,180,128]{3,2,1,0:T(8,128)(2,1)} %copy.143) | data formatting | bytes 737280 | tf_op jit(solution)/shard_map/reshape | solution.py:36
  57.6 1.3 %fusion.76 = f32[1440,128]{1,0:T(8,128)S(1)} fusion(bf16[1440,128]{1,0:T(8,128)(2,1)} %reshape.283, bf16[9,128,128]{2,1,0:T(8,128)(2,1)} %param.17), kind=kOutput, calls=%fused_computation.134 | convolution fusion | flops 47185920 | bytes 1138688 | tf_op jit(solution)/shard_map/dot_general | solution.py:39
  58.9 1.3 %convolution_add_fusion.7 = f32[1440,128]{1,0:T(8,128)S(1)} fusion(f32[1440,128]{1,0:T(8,128)S(1)} %fusion.76, bf16[1440,128]{1,0:T(8,128)(2,1)} %reshape.284, bf16[9,128,128]{2,1,0:T(8,128)(2,1)} %param.17), kind=kOutput, calls=%fused_computation.10 | convolution fusion | flops 47370240 | bytes 1875968 | tf_op jit(solution)/shard_map/dot_general | solution.py:39
  64.6 1.0 constant_dynamic-update-slice_fusion.2
  67.1 1.1 convolution_add_fusion.15
  69.6 1.9 %fusion.5 = f32[360,256]{1,0:T(8,128)} fusion(f32[360,256]{1,0:T(8,128)S(1)} %fusion.24, f32[360,256]{1,0:T(8,128)S(1)} %convolution_add_fusion.10, bf16[1,1,360,256]{3,2,1,0:T(8,128)(2,1)} %collective-permute-done.1, bf16[9,256,256]{2,1,0:T(8,128)(2,1)S(1)} %copy-done.13), kind=kOutput, calls=%fused_computation.33 | convolution fusion | flops 47370240 | bytes 1421312 | tf_op jit(solution)/shard_map/dot_general | solution.py:39
  71.5 4.3 %all-to-all-start = ((bf16[1,4,2,180,128]{4,2,3,0,1:T(2,128)(2,1)}), bf16[1,4,2,180,128]{4,2,3,0,1:T(2,128)(2,1)}, u32[]{:S(2)}, u32[]{:S(2)}) async-start(bf16[1,4,2,180,128]{4,2,3,0,1:T(2,128)(2,1)} %copy.131), calls=%async_computation | async-start | bytes 737280 | tf_op jit(solution)/shard_map/all_to_all | solution.py:250
  75.8 1.2 %copy_convert_fusion = f32[1,4,2,180,128]{4,1,3,2,0:T(4,128)S(1)} fusion(bf16[1,4,2,180,128]{4,2,3,0,1:T(2,128)(2,1)} %all-to-all-done.1), kind=kLoop, calls=%fused_computation.83 | loop fusion | flops 184320 | bytes 1105920 | tf_op jit(solution)/shard_map/convert_element_type | solution.py:300
  77.1 1.3 %multiply_convert_fusion = (bf16[1,8,180,128]{3,2,1,0:T(8,128)(2,1)S(1)}, f32[1,8,180,128]{3,2,1,0:T(8,128)}) fusion(bf16[1,8,180,128]{3,1,2,0:T(8,128)(2,1)S(1)} %copy-done.18, f32[8,180]{1,0:T(8,128)S(1)} %convert_element_type.92, f32[1,8,180,128]{3,2,1,0:T(8,128)S(1)} %copy-done.2, f32[1,8,180,128]{3,2,1,0:T(8,128)S(1)} %bitcast.192, ...), kind=kLoop, calls=%fused_computation.55 | loop fusion | flops 2949120 | bytes 3323520 | tf_op jit(solution)/shard_map/convert_element_type | solution.py:303
  78.5 1.0 fusion.11
  79.5 1.1 fusion.10
  80.6 1.1 fusion.9
  81.6 1.4 %all-to-all-done = bf16[1,4,2,180,128]{4,2,3,0,1:T(2,128)(2,1)} async-done(((bf16[1,4,2,180,128]{4,2,3,0,1:T(2,128)(2,1)}), bf16[1,4,2,180,128]{4,2,3,0,1:T(2,128)(2,1)}, u32[]{:S(2)}, u32[]{:S(2)}) %all-to-all-start) | async-done | bytes 368672 | tf_op jit(solution)/shard_map/all_to_all | solution.py:250
  83.0 1.0 copy.132
  84.2 3.4 %gather_fusion = bf16[1440,128]{1,0:T(8,128)(2,1)S(1)} fusion(bf16[1440,128]{1,0:T(8,128)(2,1)S(1)} %reshape.305, s32[2048]{0:T(1024)S(1)} %pad_clamp_fusion.1), kind=kCustom, calls=%fused_computation | custom fusion | bytes 743040 | tf_op jit(solution)/shard_map/jit(_take)/gather | solution.py:283
  87.6 2.1 %multiply_reduce_fusion.1 = bf16[360,128]{1,0:T(8,128)(2,1)S(1)} fusion(f32[360,4]{1,0:T(8,128)S(1)} %copy-done.14, bf16[1,1,360,4,128]{4,3,2,1,0:T(4,128)(2,1)S(1)} %bitcast.194, pred[360,4]{1,0:T(8,128)(4,1)S(1)} %copy-done.21), kind=kLoop, calls=%fused_computation.59 | loop fusion | flops 691200 | bytes 468000 | tf_op jit(solution)/shard_map/reduce_sum | solution.py:288
  89.7 1.1 fusion.21
  92.2 24.5 %shard_map.156 = (f32[9,32,64]{2,1,0:T(8,128)S(1)}, f32[9,16,32]{2,1,0:T(8,128)S(1)}) custom-call(bf16[3,256,768]{2,1,0:T(8,128)(2,1)S(1)} %pad_maximum_fusion.3.ga_ref, bf16[3,128,384]{2,1,0:T(8,128)(2,1)S(1)} %pad_maximum_fusion.6.go_ref), custom_call_target="tpu_custom_call" | custom-call | tf_op jit(solution)/shard_map/pallas_call | solution.py:191
  (121 shorter events, 22.4 us)
Async XLA Ops:
  0.6 89.0 %copy-start = (bf16[128,256]{1,0:T(8,128)(2,1)S(1)}, bf16[128,256]{1,0:T(8,128)(2,1)}, u32[]{:S(2)}) copy-start(bf16[128,256]{1,0:T(8,128)(2,1)} %param.19) | copy-start | bytes 196612
  0.6 64.0 %collective-permute-start = (bf16[1,1,360,256]{3,2,1,0:T(8,128)(2,1)}, bf16[1,1,360,256]{3,2,1,0:T(8,128)(2,1)}, u32[]{:S(2)}, u32[]{:S(2)}) collective-permute-start(bf16[1,1,360,256]{3,2,1,0:T(8,128)(2,1)} %param.13), channel_id=1, source_target_pairs={{0,1},{1,2},{2,3},{4,5},{5,6},{6,7},{8,9},{9,10},{10,11},{12,13},{... | collective-permute-start | bytes 552968 | tf_op jit(solution)/shard_map/ppermute | solution.py:19
  3.8 61.9 %collective-permute-start.1 = (bf16[1,1,360,256]{3,2,1,0:T(8,128)(2,1)}, bf16[1,1,360,256]{3,2,1,0:T(8,128)(2,1)}, u32[]{:S(2)}, u32[]{:S(2)}) collective-permute-start(bf16[1,1,360,256]{3,2,1,0:T(8,128)(2,1)} %param.13), channel_id=1, source_target_pairs={{1,0},{2,1},{3,2},{5,4},{6,5},{7,6},{9,8},{10,9},{11,10},{13,12},{... | collective-permute-start | bytes 552968 | tf_op jit(solution)/shard_map/ppermute | solution.py:21
  6.2 35.1 %collective-permute-start.2 = (bf16[1,8,1,128]{3,2,1,0:T(2,128)(2,1)S(1)}, bf16[1,8,1,128]{3,2,1,0:T(2,128)(2,1)S(1)}, u32[]{:S(2)}, u32[]{:S(2)}) collective-permute-start(bf16[1,8,1,128]{3,2,1,0:T(2,128)(2,1)S(1)} %get-tuple-element.47), channel_id=1, source_target_pairs={{0,1},{1,2},{2,3},{3,0},{4,5},{5,6},{6,7},{7,4},{8,9},{9,10},{10,1... | collective-permute-start | bytes 6152 | tf_op jit(solution)/shard_map/ppermute | solution.py:19
  8.8 32.5 %collective-permute-start.3 = (bf16[1,8,1,128]{3,2,1,0:T(2,128)(2,1)S(1)}, bf16[1,8,1,128]{3,2,1,0:T(2,128)(2,1)S(1)}, u32[]{:S(2)}, u32[]{:S(2)}) collective-permute-start(bf16[1,8,1,128]{3,2,1,0:T(2,128)(2,1)S(1)} %get-tuple-element.48), channel_id=1, source_target_pairs={{1,0},{2,1},{3,2},{0,3},{5,4},{6,5},{7,6},{4,7},{9,8},{10,9},{11,1... | collective-permute-start | bytes 6152 | tf_op jit(solution)/shard_map/ppermute | solution.py:21
  10.8 1.0 copy-start.23
  32.2 5.3 %copy-start.26 = (s32[1,360,4]{1,2,0:T(4,128)S(1)}, s32[1,360,4]{1,2,0:T(4,128)}, u32[]{:S(2)}) copy-start(s32[1,360,4]{1,2,0:T(4,128)} %param.22) | copy-start | bytes 17284
  32.2 6.5 %copy-start.24 = (s32[8,180]{1,0:T(8,128)S(1)}, s32[8,180]{1,0:T(8,128)}, u32[]{:S(2)}) copy-start(s32[8,180]{1,0:T(8,128)} %param.15) | copy-start | bytes 17284
  32.2 6.5 %copy-start.1 = (bf16[1,8,180,128]{3,1,2,0:T(8,128)(2,1)S(1)}, bf16[1,8,180,128]{3,1,2,0:T(8,128)(2,1)}, u32[]{:S(2)}) copy-start(bf16[1,8,180,128]{3,1,2,0:T(8,128)(2,1)} %param.14) | copy-start | bytes 1105924
  33.3 7.2 %copy-start.25 = (f32[1,360,4]{1,2,0:T(4,128)S(1)}, f32[1,360,4]{1,2,0:T(4,128)}, u32[]{:S(2)}) copy-start(f32[1,360,4]{1,2,0:T(4,128)} %param.23) | copy-start | bytes 17284
  33.3 38.2 %all-to-all-start.1 = ((bf16[1,4,2,180,128]{4,2,3,0,1:T(2,128)(2,1)}), bf16[1,4,2,180,128]{4,2,3,0,1:T(2,128)(2,1)}, u32[]{:S(2)}, u32[]{:S(2)}) async-start(bf16[1,4,2,180,128]{4,2,3,0,1:T(2,128)(2,1)} %copy.146), calls=%async_computation.1 | async-start | bytes 737280 | tf_op jit(solution)/shard_map/all_to_all | solution.py:269
  57.6 2.6 %copy-start.7 = (bf16[1440,128]{1,0:T(8,128)(2,1)S(1)}, bf16[1440,128]{1,0:T(8,128)(2,1)}, u32[]{:S(2)}) copy-start(bf16[1440,128]{1,0:T(8,128)(2,1)} %reshape.285) | copy-start | bytes 1105924
  57.6 2.6 %copy-start.20 = (bf16[9,128,128]{2,1,0:T(8,128)(2,1)S(1)}, bf16[9,128,128]{2,1,0:T(8,128)(2,1)}, u32[]{:S(2)}) copy-start(bf16[9,128,128]{2,1,0:T(8,128)(2,1)} %param.17) | copy-start | bytes 884740
  58.9 1.6 %copy-start.12 = (bf16[1440,128]{1,0:T(8,128)(2,1)S(1)}, bf16[1440,128]{1,0:T(8,128)(2,1)}, u32[]{:S(2)}) copy-start(bf16[1440,128]{1,0:T(8,128)(2,1)} %reshape.286) | copy-start | bytes 1105924
  60.2 1.0 copy-start.6
  60.5 1.0 copy-start.11
  61.2 1.0 copy-start.10
  61.5 1.0 copy-start.8
  62.2 1.0 copy-start.9
  64.4 2.3 %copy-start.13 = (bf16[9,256,256]{2,1,0:T(8,128)(2,1)S(1)}, bf16[9,256,256]{2,1,0:T(8,128)(2,1)}, u32[]{:S(2)}) copy-start(bf16[9,256,256]{2,1,0:T(8,128)(2,1)} %param.16) | copy-start | bytes 3538948
  71.5 11.5 %all-to-all-start = ((bf16[1,4,2,180,128]{4,2,3,0,1:T(2,128)(2,1)}), bf16[1,4,2,180,128]{4,2,3,0,1:T(2,128)(2,1)}, u32[]{:S(2)}, u32[]{:S(2)}) async-start(bf16[1,4,2,180,128]{4,2,3,0,1:T(2,128)(2,1)} %copy.131), calls=%async_computation | async-start | bytes 737280 | tf_op jit(solution)/shard_map/all_to_all | solution.py:250
  75.8 1.3 %copy-start.2 = (f32[1,8,180,128]{3,2,1,0:T(8,128)S(1)}, f32[1,8,180,128]{3,2,1,0:T(8,128)}, u32[]{:S(2)}) copy-start(f32[1,8,180,128]{3,2,1,0:T(8,128)} %reshape.292) | copy-start | bytes 2211844
  75.8 1.3 %copy-start.18 = (bf16[1,8,180,128]{3,1,2,0:T(8,128)(2,1)S(1)}, bf16[1,8,180,128]{3,1,2,0:T(8,128)(2,1)}, u32[]{:S(2)}) copy-start(bf16[1,8,180,128]{3,1,2,0:T(8,128)(2,1)} %param.25) | copy-start | bytes 1105924
  84.1 3.4 %copy-start.14 = (f32[360,4]{1,0:T(8,128)S(1)}, f32[360,4]{1,0:T(8,128)}, u32[]{:S(2)}) copy-start(f32[360,4]{1,0:T(8,128)} %copy.134) | copy-start | bytes 17284
  84.1 3.4 %copy-start.21 = (pred[360,4]{1,0:T(8,128)(4,1)S(1)}, pred[360,4]{1,0:T(8,128)(4,1)}, u32[]{:S(2)}) copy-start(pred[360,4]{1,0:T(8,128)(4,1)} %copy.129) | copy-start | bytes 4324
  84.2 5.5 %copy-start.5 = (bf16[1,1,360,256]{3,2,1,0:T(8,128)(2,1)S(1)}, bf16[1,1,360,256]{3,2,1,0:T(8,128)(2,1)}, u32[]{:S(2)}) copy-start(bf16[1,1,360,256]{3,2,1,0:T(8,128)(2,1)} %param.13) | copy-start | bytes 552964
  84.2 5.5 %copy-start.19 = (f32[360,256]{1,0:T(8,128)S(1)}, f32[360,256]{1,0:T(8,128)}, u32[]{:S(2)}) copy-start(f32[360,256]{1,0:T(8,128)} %fusion.5) | copy-start | bytes 1105924
  84.2 5.5 %copy-start.27 = (bf16[1,1,360,256]{3,2,1,0:T(8,128)(2,1)S(1)}, bf16[1,1,360,256]{3,2,1,0:T(8,128)(2,1)}, u32[]{:S(2)}) copy-start(bf16[1,1,360,256]{3,2,1,0:T(8,128)(2,1)} %param.24) | copy-start | bytes 552964
  90.8 1.2 %copy-start.15 = (bf16[1,128,384]{2,1,0:T(8,128)(2,1)S(1)}, bf16[1,128,384]{2,1,0:T(8,128)(2,1)}, u32[]{:S(2)}) copy-start(bf16[1,128,384]{2,1,0:T(8,128)(2,1)} %fusion.11) | copy-start | bytes 294916
  90.8 1.2 %copy-start.16 = (bf16[1,128,384]{2,1,0:T(8,128)(2,1)S(1)}, bf16[1,128,384]{2,1,0:T(8,128)(2,1)}, u32[]{:S(2)}) copy-start(bf16[1,128,384]{2,1,0:T(8,128)(2,1)} %fusion.10) | copy-start | bytes 294916
  90.8 1.2 %copy-start.17 = (bf16[1,128,384]{2,1,0:T(8,128)(2,1)S(1)}, bf16[1,128,384]{2,1,0:T(8,128)(2,1)}, u32[]{:S(2)}) copy-start(bf16[1,128,384]{2,1,0:T(8,128)(2,1)} %fusion.9) | copy-start | bytes 294916
  92.1 24.7 %copy-start.3 = (f32[1,8,180,128]{3,2,1,0:T(8,128)S(1)}, f32[1,8,180,128]{3,2,1,0:T(8,128)}, u32[]{:S(2)}) copy-start(f32[1,8,180,128]{3,2,1,0:T(8,128)} %get-tuple-element.35) | copy-start | bytes 2211844
  (2 other events, 1.9 us)

commit v2 on v1

--- a/solution.py
+++ b/solution.py
@@ -74,23 +74,152 @@
     )
 
 
-def reduce_kernel(
-    samples, ga_ref, go_ref, outa_ref, outo_ref, r1a, r1o, s2a, s2o, r2a, r2o, da, r4, sems
+def two_parts(value):
+    high = value.astype(jnp.bfloat16)
+    return high, (value - high.astype(jnp.float32)).astype(jnp.bfloat16)
+
+
+def picked(ids, factors, first, cells):
+    extent = cells.shape[0]
+    place = lax.broadcasted_iota(jnp.int32, (extent, ids.shape[1]), 0) + first
+    shares = jnp.zeros(place.shape, jnp.float32)
+    for k in range(ids.shape[0]):
+        shares = shares + jnp.where(place == ids[k : k + 1], factors[k : k + 1], 0.0)
+    return sum(turned_dot(part, cells) for part in two_parts(shares))
+
+
+def turned_dot(left, right):
+    return lax.dot_general(
+        left, right, (((0,), (0,)), ((), ())), preferred_element_type=jnp.float32
+    )
+
+
+def step_kernel(
+    samples,
+    x_ref, p_ref, wet_ref, wa_ref, wo_ref, emit_ref, drive_ref,
+    rid_ref, rfac_ref, tid_ref, tfac_ref, cota_ref, coto_ref,
+    nexta_ref, nexto_ref, outa_ref, outo_ref,
+    hal, xo, fs, fi, hs, hr, ax, xca, pp, xco, dea, deo, ga_ref, go_ref,
+    r1a, r1o, s2a, s2o, r2a, r2o, da, r4, sems, near,
 ):
     comp = lax.axis_index("comp")
     dp = lax.axis_index("dp")
+    bands = 4
+    rows, lons = p_ref.shape[0], p_ref.shape[1]
+    cells = x_ref.shape[0]
     core = lax.rem(comp, 2)
     half = comp // 2
     twin = {"comp": 2 * half + 1 - core}
     across = {"comp": 2 * (1 - half) + core}
     barrier = pltpu.get_barrier_semaphore()
-    pl.semaphore_signal(barrier, inc=1, device_id=twin, device_id_type=MESH)
-    pl.semaphore_signal(barrier, inc=1, device_id=across, device_id_type=MESH)
+    for k in range(1, bands):
+        pl.semaphore_signal(
+            barrier, inc=1, device_id={"comp": lax.rem(comp + k, bands)}, device_id_type=MESH
+        )
     for k in range(1, samples):
         pl.semaphore_signal(
             barrier, inc=1, device_id={"dp": lax.rem(dp + k, samples)}, device_id_type=MESH
         )
-    pl.semaphore_wait(barrier, samples + 1)
+    pl.semaphore_wait(barrier, samples + bands - 2)
+    up = {"comp": lax.rem(comp + 1, bands)}
+    down = {"comp": lax.rem(comp + bands - 1, bands)}
+    halos = [
+        remote(x_ref, hal.at[0], near, 0, up),
+        remote(x_ref, hal.at[1], near, 1, down),
+    ]
+    swaps = []
+    for k in range(1, bands):
+        peer = lax.rem(comp + k, bands)
+        swaps.append(
+            remote(
+                p_ref.at[pl.ds(2 * peer, 2)],
+                xo.at[pl.ds(2 * comp, 2)],
+                near,
+                3 + k,
+                {"comp": peer},
+            )
+        )
+    for copy in halos + swaps:
+        copy.start()
+    pp[...] = jnp.zeros_like(pp)
+    for r in range(rows):
+        pp[r, 8 : 8 + lons, :] = p_ref[r].astype(jnp.float32)
+    hs[0] = pp[:, 7 + lons : 8 + lons, :]
+    hs[1] = pp[:, 8:9, :]
+    sides = [remote(hs.at[0], hr.at[0], near, 2, up), remote(hs.at[1], hr.at[1], near, 3, down)]
+    for copy in sides:
+        copy.start()
+    flux_cells = jnp.dot(
+        x_ref[...], emit_ref[...], preferred_element_type=jnp.float32
+    ).astype(jnp.bfloat16)
+    fluxes = []
+    for k in (1, 2, 3, 0):
+        peer = lax.rem(comp + k, bands)
+        for r in range(2):
+            value = picked(
+                rid_ref[2 * peer + r], rfac_ref[2 * peer + r], comp * cells, flux_cells
+            ).astype(jnp.bfloat16)
+            if k:
+                fs[2 * (k - 1) + r] = value
+            else:
+                fi[2 * comp + r] = value
+        if k:
+            copy = remote(
+                fs.at[pl.ds(2 * (k - 1), 2)],
+                fi.at[pl.ds(2 * comp, 2)],
+                near,
+                6 + k,
+                {"comp": peer},
+            )
+            copy.start()
+            fluxes.append(copy)
+    xo[pl.ds(2 * comp, 2)] = p_ref[pl.ds(2 * comp, 2)]
+    wide = x_ref.shape[1]
+    xca[...] = jnp.zeros_like(xca)
+    dea[...] = jnp.zeros_like(dea)
+    xco[...] = jnp.zeros_like(xco)
+    deo[...] = jnp.zeros_like(deo)
+    for a in (1, 0, 2):
+        if a == 1:
+            line = x_ref[...].astype(jnp.float32)
+        else:
+            halos[a // 2].wait_recv()
+            line = jnp.where(
+                comp == (0 if a == 0 else bands - 1), 0.0, hal[a // 2].astype(jnp.float32)
+            )
+        ax[8 : 8 + cells, :] = line
+        ax[7:8, :] = line[cells - 1 : cells]
+        ax[8 + cells : 9 + cells, :] = line[0:1]
+        for b in range(3):
+            xca[a, 0:cells, b * wide : (b + 1) * wide] = ax[7 + b : 7 + b + cells, :].astype(
+                jnp.bfloat16
+            )
+    za = jnp.dot(xca[0], wa_ref[0], preferred_element_type=jnp.float32)
+    za = za + jnp.dot(xca[1], wa_ref[1], preferred_element_type=jnp.float32)
+    za = za + jnp.dot(xca[2], wa_ref[2], preferred_element_type=jnp.float32)
+    za = za[:cells]
+    for copy in swaps:
+        copy.wait_recv()
+    total_lons = lons * bands
+    surface = jnp.zeros((cells, p_ref.shape[2]), jnp.float32)
+    for t in range(bands):
+        for r in range(2):
+            surface = surface + picked(
+                tid_ref[...],
+                tfac_ref[...],
+                (2 * comp + r) * total_lons + t * lons,
+                xo[2 * t + r],
+            )
+    za = za + jnp.dot(
+        surface.astype(jnp.bfloat16), drive_ref[...], preferred_element_type=jnp.float32
+    )
+    gate = lax.logistic(za)
+    nexta_ref[...] = x_ref[...].astype(jnp.float32) + za * gate
+    dea[0:cells, :] = (
+        cota_ref[...].astype(jnp.float32) * (gate * (1.0 + za * (1.0 - gate)))
+    ).astype(jnp.bfloat16)
+    for a in range(3):
+        ga_ref[a] = turned_dot(dea[...], xca[a]).astype(jnp.bfloat16)
     wa = s2a.shape[1]
     wo = s2o.shape[1]
 
@@ -106,9 +235,23 @@
                 remote(block(go_ref, wo, band), r1o.at[n], sems, 2 * n + 1, twin),
             )
         )
-    for pair in first:
-        for copy in pair:
-            copy.start()
+    first[0][0].start()
+    first[1][0].start()
+
+    for copy in sides:
+        copy.wait_recv()
+    pp[:, 7:8, :] = hr[0]
+    pp[:, 8 + lons : 9 + lons, :] = hr[1]
+    thin = p_ref.shape[2]
+
+    def join(r, carry):
+        for b in range(3):
+            xco[r + 1, 0:lons, b * thin : (b + 1) * thin] = pp[
+                r, 7 + b : 7 + b + lons, :
+            ].astype(jnp.bfloat16)
+        return carry
+
+    lax.fori_loop(0, rows, join, 0)
     other = 2 * (1 - half) + core
     first[0][0].wait_recv()
     s2a[...] = (
@@ -116,6 +259,33 @@
     ).astype(jnp.bfloat16)
     second_a = remote(s2a, r2a, sems, 4, across)
     second_a.start()
+    for copy in fluxes:
+        copy.wait_recv()
+
+    def ocean(r, carry):
+        zo = jnp.dot(xco[r], wo_ref[0], preferred_element_type=jnp.float32)
+        zo = zo + jnp.dot(xco[r + 1], wo_ref[1], preferred_element_type=jnp.float32)
+        zo = zo + jnp.dot(xco[r + 2], wo_ref[2], preferred_element_type=jnp.float32)
+        zo = zo[:lons] + fi[r].astype(jnp.float32)
+        chosen = jnp.where(
+            lax.broadcasted_iota(jnp.int32, (rows, thin), 0) == r, 1.0, 0.0
+        ).astype(jnp.bfloat16)
+        wet = turned_dot(wet_ref[...].astype(jnp.float32).astype(jnp.bfloat16), chosen)
+        gate = lax.logistic(zo)
+        nexto_ref[r] = p_ref[r].astype(jnp.float32) + wet * (zo * gate)
+        deo[r, 0:lons, :] = (
+            coto_ref[r].astype(jnp.float32) * wet * (gate * (1.0 + zo * (1.0 - gate)))
+        ).astype(jnp.bfloat16)
+        return carry
+
+    lax.fori_loop(0, rows, ocean, 0)
+    delta = deo[...].reshape(-1, thin)
+    for a in range(3):
+        go_ref[a] = turned_dot(
+            delta, xco[a : a + rows].reshape(-1, 3 * thin)
+        ).astype(jnp.bfloat16)
+    first[0][1].start()
+    first[1][1].start()
     first[0][1].wait_recv()
     s2o[...] = (
         block(go_ref, wo, other)[...].astype(jnp.float32) + r1o[0].astype(jnp.float32)
@@ -169,6 +339,8 @@
     second_o.wait_send()
     for copy in third:
         copy.wait_send()
+    for copy in halos + swaps + sides + fluxes:
+        copy.wait_send()
 
 
 def plain_sum(joined):
@@ -178,47 +350,12 @@
     return lax.psum_scatter(banded, "dp", scatter_dimension=1, tiled=True)
 
 
-def summed_terms(ga, go):
-    samples = lax.axis_size("dp")
-    bands = lax.axis_size("comp")
-    wa, wo = ga.shape[1] // bands, go.shape[1] // bands
-    ca, co = ga.shape[2] // 3 // samples, go.shape[2] // 3 // samples
-    if bands != 4 or wa != 64 or wo != 32 or ca % 16 or co % 16:
-        return plain_sum(ga), plain_sum(go)
-    la, lo = ga.shape[2], go.shape[2]
-    piece = 6 * ca + 3 * co
-    vmem = pl.BlockSpec(memory_space=pltpu.VMEM)
-    return pl.pallas_call(
-        functools.partial(reduce_kernel, samples),
-        out_shape=(
-            jax.ShapeDtypeStruct((9, ca, wa), jnp.float32),
-            jax.ShapeDtypeStruct((9, co, wo), jnp.float32),
-        ),
-        in_specs=[vmem] * 2,
-        out_specs=(vmem, vmem),
-        scratch_shapes=[
-            pltpu.VMEM((2, 3, wa, la), jnp.bfloat16),
-            pltpu.VMEM((2, 3, wo, lo), jnp.bfloat16),
-            pltpu.VMEM((3, wa, la), jnp.bfloat16),
-            pltpu.VMEM((3, wo, lo), jnp.bfloat16),
-            pltpu.VMEM((3, wa, la), jnp.bfloat16),
-            pltpu.VMEM((3, wo, lo), jnp.bfloat16),
-            pltpu.VMEM((samples, piece, 128), jnp.bfloat16),
-            pltpu.VMEM((samples - 1, piece, 128), jnp.bfloat16),
-            pltpu.SemaphoreType.DMA((2, 5 + samples)),
-        ],
-        compiler_params=pltpu.CompilerParams(
-            collective_id=0, has_side_effects=True, vmem_limit_bytes=32 * 1024 * 1024
-        ),
-    )(ga.astype(jnp.bfloat16), go.astype(jnp.bfloat16))
-
-
 def silu_slope(value):
     logistic = jax.nn.sigmoid(value)
     return logistic * (1.0 + value * (1.0 - logistic))
 
 
-def per_device(
+def by_parts(
     climate_vector,
     pelagic_vector,
     wet_land_flags,
@@ -303,8 +440,98 @@
     delta_o = (upcoming_pelagic_sensitivity.astype(jnp.float32) * wet * silu_slope(zo)).astype(
         jnp.bfloat16
     )
-    summed = summed_terms(joined_terms(padded_a, delta_a), joined_terms(padded_o, delta_o))
+    summed = (
+        plain_sum(joined_terms(padded_a, delta_a)),
+        plain_sum(joined_terms(padded_o, delta_o)),
+    )
     return (atmos_next, ocean_next, summed[0], summed[1])
+
+
+def whole_step(x, p, wet, wa, wo, emit, drive, rid, rfac, tid, tfac, cota, coto):
+    samples = lax.axis_size("dp")
+    bands = lax.axis_size("comp")
+    rows, lons, thin = p.shape[1:]
+    cells, wide = x.shape[2:]
+    ca, co, va, vo = wide // samples, thin // samples, wide // bands, thin // bands
+    tall = -(-lons // 64) * 64
+    high = -(-cells // 128) * 128
+    near = rid.shape[2]
+
+    def by_band(ids):
+        return ids.reshape(2, bands, lons, near).transpose(1, 0, 3, 2).reshape(-1, near, lons)
+
+    vmem = pl.BlockSpec(memory_space=pltpu.VMEM)
+    half, full = jnp.bfloat16, jnp.float32
+    piece = 6 * ca + 3 * co
+    outs = pl.pallas_call(
+        functools.partial(step_kernel, samples),
+        out_shape=(
+            jax.ShapeDtypeStruct((cells, wide), full),
+            jax.ShapeDtypeStruct((rows, lons, thin), full),
+            jax.ShapeDtypeStruct((9, ca, va), full),
+            jax.ShapeDtypeStruct((9, co, vo), full),
+        ),
+        in_specs=[vmem] * 13,
+        out_specs=(vmem,) * 4,
+        scratch_shapes=[
+            pltpu.VMEM((2, cells, wide), half),
+            pltpu.VMEM((rows, lons, thin), half),
+            pltpu.VMEM((2 * bands - 2, lons, thin), half),
+            pltpu.VMEM((rows, lons, thin), half),
+            pltpu.VMEM((2, rows, 1, thin), full),
+            pltpu.VMEM((2, rows, 1, thin), full),
+            pltpu.VMEM((cells + 16, wide), full),
+            pltpu.VMEM((3, high, 3 * wide), half),
+            pltpu.VMEM((rows, tall + 16, thin), full),
+            pltpu.VMEM((rows + 2, tall, 3 * thin), half),
+            pltpu.VMEM((high, wide), half),
+            pltpu.VMEM((rows, tall, thin), half),
+            pltpu.VMEM((3, wide, 3 * wide), half),
+            pltpu.VMEM((3, thin, 3 * thin), half),
+            pltpu.VMEM((2, 3, va, 3 * wide), half),
+            pltpu.VMEM((2, 3, vo, 3 * thin), half),
+            pltpu.VMEM((3, va, 3 * wide), half),
+            pltpu.VMEM((3, vo, 3 * thin), half),
+            pltpu.VMEM((3, va, 3 * wide), half),
+            pltpu.VMEM((3, vo, 3 * thin), half),
+            pltpu.VMEM((samples, piece, 128), half),
+            pltpu.VMEM((samples - 1, piece, 128), half),
+            pltpu.SemaphoreType.DMA((2, 5 + samples)),
+            pltpu.SemaphoreType.DMA((2, 10)),
+        ],
+        compiler_params=pltpu.CompilerParams(
+            collective_id=0, has_side_effects=True, vmem_limit_bytes=48 * 1024 * 1024
+        ),
+    )(
+        x.reshape(cells, wide),
+        p.reshape(rows, lons, thin),
+        wet,
+        wa.reshape(3, 3 * wide, wide),
+        wo.reshape(3, 3 * thin, thin),
+        emit,
+        drive,
+        by_band(rid),
+        by_band(rfac),
+        tid.reshape(cells, -1).T,
+        tfac.reshape(cells, -1).T,
+        cota.reshape(cells, wide),
+        coto.reshape(rows, lons, thin),
+    )
+    return outs[0].reshape(x.shape), outs[1].reshape(p.shape), outs[2], outs[3]
+
+
+def per_device(*arrays):
+    x, p = arrays[0], arrays[1]
+    if (
+        lax.axis_size("comp") == 4
+        and x.shape[:2] == (1, 1)
+        and p.shape[:2] == (1, 8)
+        and x.shape[3] == 256
+        and p.shape[3] == 128
+        and p.shape[3] % (16 * lax.axis_size("dp")) == 0
+    ):
+        return whole_step(*arrays)
+    return by_parts(*arrays)
 
 
 def solution(mesh):

time: 121 us -> 48.3 us (0.40); the launches traced: 119 us -> 47.6 us
  local copies, waits for them, and re-layouts: 45.4 us -> 7.82 us
  starting transfers between devices: 16.4 us -> 0 us
  other arithmetic: 15.8 us -> 0 us
  Pallas kernels: 24.5 us -> 39 us
  matrix products: 14.3 us -> 0 us
  waiting for transfers between devices: 1.43 us -> 0 us
    gather x2 -> x0, local copies, waits for them, and re-layouts: 14.8 us -> none  [the longest x1 11.5 us: per_device(): flux_taken = jnp.take(cells_flat, local_flux, axis=1).astype(jnp.float32)]
    pallas_call x1, Pallas kernels: 24.5 us -> 39 us  [whole_step(): pl.pallas_call(functools.partial(step_kernel, samples), out_shape=(jax.Sh...]
    dot_general x26 -> x0, matrix products: 14.3 us -> none  [the longest x18 8.68 us: convolve(): jnp.dot(window, kernel[3 * tap_row + tap_col], preferred_element_type=jnp...]
    reshape x15 -> x5, local copies, waits for them, and re-layouts: 14.6 us -> 3.01 us  [the longest x4 1.8 us: by_band(): ids.reshape(2, bands, lons, near).transpose(1, 0, 3, 2)]
    reduce_sum x2 -> x0, other arithmetic: 10.6 us -> none  [the longest x1 8.5 us: per_device(): jnp.sum(flux_taken * flux_weights[None, ..., None], axis=4)]
    all_to_all x2 -> x0, starting transfers between devices: 8.53 us -> none  [the longest x1 4.28 us: per_device(): lax.all_to_all(ocean_blocks, 'comp', split_axis=1, concat_axis=1, tiled=T...]
    ppermute x4 -> x0, starting transfers between devices: 7.84 us -> none  [the longest x2 5.83 us: with_halo(): lax.ppermute(tail, axis, [(i, (i + 1) % count) for i in range(ends)])]
    slice x6 -> x0, local copies, waits for them, and re-layouts: 4.04 us -> none  [the longest x3 3.75 us: convolve(): padded[:, tap_row:tap_row + rows, tap_col:tap_col + cols].reshape(-1, width)]
  transfers between devices with their start and end apart: 6 -> 0, of which waited for: 1 -> 0; matrix products, arithmetic and copies ran while one was open for 52% -> 0% of each run, Pallas kernels for 0% -> 0%
where the time goes in v2:
time: 48.3 us; the launch traced here: 47.6 us
  Pallas kernels  39 us (81%)
  local copies, waits for them, and re-layouts  7.82 us (16%)
  between operations  0.79 us (2%)
    pallas_call x1, Pallas kernels, whole_step(): pl.pallas_call(functools.partial(step_kernel, samples), out_shape=(jax.Sh...  39 us
    unnamed x22, local copies, waits for them, and re-layouts  4.81 us
    reshape x4, local copies, waits for them, and re-layouts, by_band(): ids.reshape(2, bands, lons, near).transpose(1, 0, 3, 2)  1.8 us
    reshape x1, local copies, waits for them, and re-layouts, whole_step(): coto.reshape(rows, lons, thin)  1.2 us

profile of v2, /device:TPU:0, one launch (start us, length us, event | category | flops | bytes accessed | tf_op | source)
XLA Modules:
  0.0 47.6 jit_solution(16230042759920190747)
XLA Ops:
  0.6 0.0 copy-start.8
  0.6 0.0 copy-start.7
  0.7 0.0 copy-start.4
  0.7 0.0 copy-start.1
  0.7 0.0 copy-start
  0.7 0.0 copy-start.6
  0.7 0.0 copy-start.2
  0.7 1.0 %reshape.54 = s32[2,4,180,4]{2,1,3,0:T(4,128)S(1)} reshape(s32[2,720,4]{1,2,0:T(4,128)} %param.20) | data formatting | bytes 46080 | tf_op jit(solution)/shard_map/reshape | solution.py:461
  1.7 0.8 %reshape.56 = f32[2,4,180,4]{2,1,3,0:T(4,128)S(1)} reshape(f32[2,720,4]{1,2,0:T(4,128)} %param.21) | data formatting | bytes 46080 | tf_op jit(solution)/shard_map/reshape | solution.py:461
  2.5 1.2 %copy_bitcast_fusion = (bf16[8,180,128]{2,1,0:T(8,128)(2,1)S(1)}, bf16[8,180,128]{2,1,0:T(8,128)(2,1)S(1)}) fusion(bf16[1,8,180,128]{3,1,2,0:T(8,128)(2,1)} %param.25, bf16[1,8,180,128]{3,1,2,0:T(8,128)(2,1)} %param.14), kind=kLoop, calls=%fused_computation | loop fusion | bytes 1474560 | tf_op jit(solution)/shard_map/reshape | solution.py:518
  3.7 0.0 copy-done.8
  3.7 0.0 copy-done.7
  3.8 0.0 copy-done.4
  3.8 0.0 copy-done.1
  3.8 0.0 copy-done
  3.8 0.0 copy-done.6
  3.8 0.0 copy-done.2
  3.8 0.0 copy-start.3
  3.8 0.9 %copy-done.3 = bf16[1,1,360,256]{3,2,1,0:T(8,128)(2,1)S(1)} copy-done((bf16[1,1,360,256]{3,2,1,0:T(8,128)(2,1)S(1)}, bf16[1,1,360,256]{3,2,1,0:T(8,128)(2,1)}, u32[]{:S(2)}) %copy-start.3) | copy-done | bytes 184344
  4.7 0.0 copy-start.5
  4.7 0.8 %copy-done.5 = bf16[128,256]{1,0:T(8,128)(2,1)S(1)} copy-done((bf16[128,256]{1,0:T(8,128)(2,1)S(1)}, bf16[128,256]{1,0:T(8,128)(2,1)}, u32[]{:S(2)}) %copy-start.5) | copy-done | bytes 65560
  5.6 39.0 %shard_map.156 = (f32[360,256]{1,0:T(8,128)S(1)}, f32[8,180,128]{2,1,0:T(8,128)S(1)}, f32[9,32,64]{2,1,0:T(8,128)S(1)}, f32[9,16,32]{2,1,0:T(8,128)S(1)}) custom-call(bf16[360,256]{1,0:T(8,128)(2,1)S(1)} %bitcast.30, bf16[8,180,128]{2,1,0:T(8,128)(2,1)S(1)} %get-tuple-element.17.p_ref, s32[8,180]{1,0:T(8,128)S(1)} %copy-done.6, ...), custom_call_target="tpu_custom_call" | custom-call | tf_op jit(solution)/shard_map/pallas_call | solution.py:466
  44.6 1.0 %copy.21 = f32[1,8,180,128]{3,1,2,0:T(8,128)} copy(f32[1,8,180,128]{3,2,1,0:T(8,128)S(1)} %bitcast.27) | data formatting | bytes 1474560
  45.6 0.7 %copy.27 = f32[1,1,360,256]{3,2,1,0:T(8,128)} copy(f32[1,1,360,256]{3,2,1,0:T(8,128)S(1)} %bitcast.28) | data formatting | bytes 737280
  46.4 0.7 %copy.28 = f32[9,32,64]{2,1,0:T(8,128)} copy(f32[9,32,64]{2,1,0:T(8,128)S(1)} %get-tuple-element.24) | data formatting | bytes 147456
  47.0 0.6 %copy.29 = f32[9,16,32]{2,1,0:T(8,128)} copy(f32[9,16,32]{2,1,0:T(8,128)S(1)} %get-tuple-element.25) | data formatting | bytes 36864
  (2 shorter events, 0.0 us)
Async XLA Ops:
  0.6 3.1 %copy-start.8 = (f32[1,360,4]{1,2,0:T(4,128)S(1)}, f32[1,360,4]{1,2,0:T(4,128)}, u32[]{:S(2)}) copy-start(f32[1,360,4]{1,2,0:T(4,128)} %param.23) | copy-start | bytes 17284
  0.6 3.1 %copy-start.7 = (s32[1,360,4]{1,2,0:T(4,128)S(1)}, s32[1,360,4]{1,2,0:T(4,128)}, u32[]{:S(2)}) copy-start(s32[1,360,4]{1,2,0:T(4,128)} %param.22) | copy-start | bytes 17284
  0.7 3.1 %copy-start.4 = (bf16[256,128]{1,0:T(8,128)(2,1)S(1)}, bf16[256,128]{1,0:T(8,128)(2,1)}, u32[]{:S(2)}) copy-start(bf16[256,128]{1,0:T(8,128)(2,1)} %emit_ref.1) | copy-start | bytes 196612
  0.7 3.1 %copy-start.1 = (bf16[9,128,128]{2,1,0:T(8,128)(2,1)S(1)}, bf16[9,128,128]{2,1,0:T(8,128)(2,1)}, u32[]{:S(2)}) copy-start(bf16[9,128,128]{2,1,0:T(8,128)(2,1)} %param.17) | copy-start | bytes 884740
  0.7 3.1 %copy-start = (bf16[9,256,256]{2,1,0:T(8,128)(2,1)S(1)}, bf16[9,256,256]{2,1,0:T(8,128)(2,1)}, u32[]{:S(2)}) copy-start(bf16[9,256,256]{2,1,0:T(8,128)(2,1)} %param.16) | copy-start | bytes 3538948
  0.7 3.1 %copy-start.6 = (s32[8,180]{1,0:T(8,128)S(1)}, s32[8,180]{1,0:T(8,128)}, u32[]{:S(2)}) copy-start(s32[8,180]{1,0:T(8,128)} %wet_ref.1) | copy-start | bytes 17284
  0.7 3.1 %copy-start.2 = (bf16[1,1,360,256]{3,2,1,0:T(8,128)(2,1)S(1)}, bf16[1,1,360,256]{3,2,1,0:T(8,128)(2,1)}, u32[]{:S(2)}) copy-start(bf16[1,1,360,256]{3,2,1,0:T(8,128)(2,1)} %param.13) | copy-start | bytes 552964
  3.8 0.9 %copy-start.3 = (bf16[1,1,360,256]{3,2,1,0:T(8,128)(2,1)S(1)}, bf16[1,1,360,256]{3,2,1,0:T(8,128)(2,1)}, u32[]{:S(2)}) copy-start(bf16[1,1,360,256]{3,2,1,0:T(8,128)(2,1)} %param.24) | copy-start | bytes 552964
  4.7 0.8 %copy-start.5 = (bf16[128,256]{1,0:T(8,128)(2,1)S(1)}, bf16[128,256]{1,0:T(8,128)(2,1)}, u32[]{:S(2)}) copy-start(bf16[128,256]{1,0:T(8,128)(2,1)} %drive_ref.1) | copy-start | bytes 196612

commit v3 on v2

--- a/solution.py
+++ b/solution.py
@@ -100,7 +100,7 @@
     rid_ref, rfac_ref, tid_ref, tfac_ref, cota_ref, coto_ref,
     nexta_ref, nexto_ref, outa_ref, outo_ref,
     hal, xo, fs, fi, hs, hr, ax, xca, pp, xco, dea, deo, ga_ref, go_ref,
-    r1a, r1o, s2a, s2o, r2a, r2o, da, r4, sems, near,
+    r1a, r1o, s2a, s2o, r2a, r2o, da, do, r4a, r4o, sems, near,
 ):
     comp = lax.axis_index("comp")
     dp = lax.axis_index("dp")
@@ -149,30 +149,6 @@
     sides = [remote(hs.at[0], hr.at[0], near, 2, up), remote(hs.at[1], hr.at[1], near, 3, down)]
     for copy in sides:
         copy.start()
-    flux_cells = jnp.dot(
-        x_ref[...], emit_ref[...], preferred_element_type=jnp.float32
-    ).astype(jnp.bfloat16)
-    fluxes = []
-    for k in (1, 2, 3, 0):
-        peer = lax.rem(comp + k, bands)
-        for r in range(2):
-            value = picked(
-                rid_ref[2 * peer + r], rfac_ref[2 * peer + r], comp * cells, flux_cells
-            ).astype(jnp.bfloat16)
-            if k:
-                fs[2 * (k - 1) + r] = value
-            else:
-                fi[2 * comp + r] = value
-        if k:
-            copy = remote(
-                fs.at[pl.ds(2 * (k - 1), 2)],
-                fi.at[pl.ds(2 * comp, 2)],
-                near,
-                6 + k,
-                {"comp": peer},
-            )
-            copy.start()
-            fluxes.append(copy)
     xo[pl.ds(2 * comp, 2)] = p_ref[pl.ds(2 * comp, 2)]
     wide = x_ref.shape[1]
     xca[...] = jnp.zeros_like(xca)
@@ -237,7 +213,30 @@
         )
     first[0][0].start()
     first[1][0].start()
-
+    flux_cells = jnp.dot(
+        x_ref[...], emit_ref[...], preferred_element_type=jnp.float32
+    ).astype(jnp.bfloat16)
+    for t in range(bands):
+        for r in range(2):
+            fs[2 * t + r] = picked(
+                rid_ref[r, :, t * lons : (t + 1) * lons],
+                rfac_ref[r, :, t * lons : (t + 1) * lons],
+                comp * cells,
+                flux_cells,
+            ).astype(jnp.bfloat16)
+    fluxes = []
+    for k in range(1, bands):
+        peer = lax.rem(comp + k, bands)
+        copy = remote(
+            fs.at[pl.ds(2 * peer, 2)],
+            fi.at[pl.ds(2 * comp, 2)],
+            near,
+            6 + k,
+            {"comp": peer},
+        )
+        copy.start()
+        fluxes.append(copy)
+    fi[pl.ds(2 * comp, 2)] = fs[pl.ds(2 * comp, 2)]
     for copy in sides:
         copy.wait_recv()
     pp[:, 7:8, :] = hr[0]
@@ -279,6 +278,26 @@
         return carry
 
     lax.fori_loop(0, rows, ocean, 0)
+    first[1][0].wait_recv()
+    own_a = block(ga_ref, wa, comp)[...].astype(jnp.float32) + r1a[1].astype(jnp.float32)
+    second_a.wait_recv()
+    own_a = own_a + r2a[...].astype(jnp.float32)
+    ca = outa_ref.shape[1]
+    co = outo_ref.shape[1]
+    ta = own_a.reshape(3 * wa, -1)
+    ta = jnp.concatenate([ta, jnp.zeros((wa, ta.shape[1]), jnp.float32)], axis=0).T
+    ta = ta.astype(jnp.bfloat16)
+    for d in range(samples):
+        for b in range(3):
+            piece = ta[(b * samples + d) * ca : (b * samples + d + 1) * ca]
+            da[d, b * ca : (b + 1) * ca, :] = piece[:, :128]
+            da[d, (3 + b) * ca : (4 + b) * ca, :] = piece[:, 128:]
+    third_a = []
+    for k in range(1, samples):
+        peer = lax.rem(dp + k, samples)
+        copy = remote(da.at[peer], r4a.at[k - 1], sems, 5 + k, {"dp": peer})
+        copy.start()
+        third_a.append(copy)
     delta = deo[...].reshape(-1, thin)
     for a in range(3):
         go_ref[a] = turned_dot(
@@ -292,52 +311,45 @@
     ).astype(jnp.bfloat16)
     second_o = remote(s2o, r2o, sems, 5, across)
     second_o.start()
-    first[1][0].wait_recv()
     first[1][1].wait_recv()
-    own_a = block(ga_ref, wa, comp)[...].astype(jnp.float32) + r1a[1].astype(jnp.float32)
     own_o = block(go_ref, wo, comp)[...].astype(jnp.float32) + r1o[1].astype(jnp.float32)
-    second_a.wait_recv()
-    own_a = own_a + r2a[...].astype(jnp.float32)
     second_o.wait_recv()
     own_o = own_o + r2o[...].astype(jnp.float32)
-    ca = outa_ref.shape[1]
-    co = outo_ref.shape[1]
-    ta = own_a.reshape(3 * wa, -1)
-    ta = jnp.concatenate([ta, jnp.zeros((wa, ta.shape[1]), jnp.float32)], axis=0).T
     to = own_o.reshape(3 * wo, -1)
     to = jnp.concatenate([to, jnp.zeros((wo, to.shape[1]), jnp.float32)], axis=0).T
-    ta = ta.astype(jnp.bfloat16)
     to = to.astype(jnp.bfloat16)
     for d in range(samples):
         for b in range(3):
-            piece = ta[(b * samples + d) * ca : (b * samples + d + 1) * ca]
-            da[d, b * ca : (b + 1) * ca, :] = piece[:, :128]
-            da[d, (3 + b) * ca : (4 + b) * ca, :] = piece[:, 128:]
-            da[d, 6 * ca + b * co : 6 * ca + (b + 1) * co, :] = to[
+            do[d, b * co : (b + 1) * co, :] = to[
                 (b * samples + d) * co : (b * samples + d + 1) * co
             ]
-    third = []
+    third_o = []
     for k in range(1, samples):
         peer = lax.rem(dp + k, samples)
-        copy = remote(da.at[peer], r4.at[k - 1], sems, 5 + k, {"dp": peer})
+        copy = remote(do.at[peer], r4o.at[k - 1], sems, 4 + samples + k, {"dp": peer})
         copy.start()
-        third.append(copy)
+        third_o.append(copy)
     total = da[dp].astype(jnp.float32)
-    for copy, k in zip(third, range(samples)):
-        copy.wait_recv()
-        total = total + r4[k].astype(jnp.float32)
+    for k in range(samples - 1):
+        third_a[k].wait_recv()
+        total = total + r4a[k].astype(jnp.float32)
     for a in range(3):
         for b in range(3):
             row = b * ca + (a // 2) * 3 * ca
             outa_ref[3 * a + b] = total[row : row + ca, (a % 2) * wa : (a % 2 + 1) * wa]
-            row = 6 * ca + b * co
-            outo_ref[3 * a + b] = total[row : row + co, a * wo : (a + 1) * wo]
+    total = do[dp].astype(jnp.float32)
+    for k in range(samples - 1):
+        third_o[k].wait_recv()
+        total = total + r4o[k].astype(jnp.float32)
+    for a in range(3):
+        for b in range(3):
+            outo_ref[3 * a + b] = total[b * co : (b + 1) * co, a * wo : (a + 1) * wo]
     for pair in first:
         for copy in pair:
             copy.wait_send()
     second_a.wait_send()
     second_o.wait_send()
-    for copy in third:
+    for copy in third_a + third_o:
         copy.wait_send()
     for copy in halos + swaps + sides + fluxes:
         copy.wait_send()
@@ -455,14 +467,9 @@
     ca, co, va, vo = wide // samples, thin // samples, wide // bands, thin // bands
     tall = -(-lons // 64) * 64
     high = -(-cells // 128) * 128
-    near = rid.shape[2]
-
-    def by_band(ids):
-        return ids.reshape(2, bands, lons, near).transpose(1, 0, 3, 2).reshape(-1, near, lons)
 
     vmem = pl.BlockSpec(memory_space=pltpu.VMEM)
     half, full = jnp.bfloat16, jnp.float32
-    piece = 6 * ca + 3 * co
     outs = pl.pallas_call(
         functools.partial(step_kernel, samples),
         out_shape=(
@@ -476,7 +483,7 @@
         scratch_shapes=[
             pltpu.VMEM((2, cells, wide), half),
             pltpu.VMEM((rows, lons, thin), half),
-            pltpu.VMEM((2 * bands - 2, lons, thin), half),
+            pltpu.VMEM((2 * bands, lons, thin), half),
             pltpu.VMEM((rows, lons, thin), half),
             pltpu.VMEM((2, rows, 1, thin), full),
             pltpu.VMEM((2, rows, 1, thin), full),
@@ -494,9 +501,11 @@
             pltpu.VMEM((3, vo, 3 * thin), half),
             pltpu.VMEM((3, va, 3 * wide), half),
             pltpu.VMEM((3, vo, 3 * thin), half),
-            pltpu.VMEM((samples, piece, 128), half),
-            pltpu.VMEM((samples - 1, piece, 128), half),
-            pltpu.SemaphoreType.DMA((2, 5 + samples)),
+            pltpu.VMEM((samples, 6 * ca, 128), half),
+            pltpu.VMEM((samples, 3 * co, 128), half),
+            pltpu.VMEM((samples - 1, 6 * ca, 128), half),
+            pltpu.VMEM((samples - 1, 3 * co, 128), half),
+            pltpu.SemaphoreType.DMA((2, 4 + 2 * samples)),
             pltpu.SemaphoreType.DMA((2, 10)),
         ],
         compiler_params=pltpu.CompilerParams(
@@ -510,8 +519,8 @@
         wo.reshape(3, 3 * thin, thin),
         emit,
         drive,
-        by_band(rid),
-        by_band(rfac),
+        rid.transpose(0, 2, 1),
+        rfac.transpose(0, 2, 1),
         tid.reshape(cells, -1).T,
         tfac.reshape(cells, -1).T,
         cota.reshape(cells, wide),

time: 48.3 us -> 56.3 us (1.17)
  Pallas kernels: 39 us -> 44.9 us
  local copies, waits for them, and re-layouts: 7.82 us -> 10.2 us
    pallas_call x1, Pallas kernels: 39 us -> 44.9 us  [whole_step(): pl.pallas_call(functools.partial(step_kernel, samples), out_shape=(jax.Sh...]
    unnamed x22 -> x26, local copies, waits for them, and re-layouts: 4.81 us -> 8.92 us
    reshape x4 -> x0, local copies, waits for them, and re-layouts: 1.8 us -> none  [by_band(): ids.reshape(2, bands, lons, near).transpose(1, 0, 3, 2)]
where the time goes in v3:
time: 56.3 us; the launch traced here: 55.9 us
  Pallas kernels  44.9 us (80%)
  local copies, waits for them, and re-layouts  10.2 us (18%)
  between operations  0.7 us (1%)
    pallas_call x1, Pallas kernels, whole_step(): pl.pallas_call(functools.partial(step_kernel, samples), out_shape=(jax.Sh...  44.9 us
    unnamed x26, local copies, waits for them, and re-layouts  8.92 us
    reshape x1, local copies, waits for them, and re-layouts, whole_step(): coto.reshape(rows, lons, thin)  1.31 us

profile of v3, /device:TPU:0, one launch (start us, length us, event | category | flops | bytes accessed | tf_op | source)
XLA Modules:
  0.0 55.9 jit_solution(4683861783668167378)
XLA Ops:
  0.6 0.0 copy-start.6
  0.6 0.0 copy-start.1
  0.7 0.0 copy-start
  0.7 0.0 copy-start.8
  0.7 1.3 %copy_bitcast_fusion = (bf16[8,180,128]{2,1,0:T(8,128)(2,1)S(1)}, bf16[8,180,128]{2,1,0:T(8,128)(2,1)S(1)}) fusion(bf16[1,8,180,128]{3,1,2,0:T(8,128)(2,1)} %param.25, bf16[1,8,180,128]{3,1,2,0:T(8,128)(2,1)} %param.14), kind=kLoop, calls=%fused_computation | loop fusion | bytes 1474560 | tf_op jit(solution)/shard_map/reshape | solution.py:527
  2.0 0.0 copy-done.6
  2.0 0.0 copy-done.1
  2.0 0.2 copy-done
  2.2 0.0 copy-done.8
  2.2 0.0 copy-start.2
  2.2 0.9 %copy-done.2 = bf16[1,1,360,256]{3,2,1,0:T(8,128)(2,1)S(1)} copy-done((bf16[1,1,360,256]{3,2,1,0:T(8,128)(2,1)S(1)}, bf16[1,1,360,256]{3,2,1,0:T(8,128)(2,1)}, u32[]{:S(2)}) %copy-start.2) | copy-done | bytes 184344
  3.2 0.0 copy-start.3
  3.2 0.9 %copy-done.3 = bf16[1,1,360,256]{3,2,1,0:T(8,128)(2,1)S(1)} copy-done((bf16[1,1,360,256]{3,2,1,0:T(8,128)(2,1)S(1)}, bf16[1,1,360,256]{3,2,1,0:T(8,128)(2,1)}, u32[]{:S(2)}) %copy-start.3) | copy-done | bytes 184344
  4.1 0.0 copy-start.4
  4.1 0.8 %copy-done.4 = bf16[256,128]{1,0:T(8,128)(2,1)S(1)} copy-done((bf16[256,128]{1,0:T(8,128)(2,1)S(1)}, bf16[256,128]{1,0:T(8,128)(2,1)}, u32[]{:S(2)}) %copy-start.4) | copy-done | bytes 65560
  4.9 0.0 copy-start.5
  4.9 0.8 %copy-done.5 = bf16[128,256]{1,0:T(8,128)(2,1)S(1)} copy-done((bf16[128,256]{1,0:T(8,128)(2,1)S(1)}, bf16[128,256]{1,0:T(8,128)(2,1)}, u32[]{:S(2)}) %copy-start.5) | copy-done | bytes 65560
  5.8 0.0 copy-start.7
  5.8 0.7 %copy-done.7 = f32[2,720,4]{1,2,0:T(4,128)S(1)} copy-done((f32[2,720,4]{1,2,0:T(4,128)S(1)}, f32[2,720,4]{1,2,0:T(4,128)}, u32[]{:S(2)}) %copy-start.7) | copy-done | bytes 23064
  6.5 0.0 copy-start.9
  6.5 0.7 %copy-done.9 = s32[1,360,4]{1,2,0:T(4,128)S(1)} copy-done((s32[1,360,4]{1,2,0:T(4,128)S(1)}, s32[1,360,4]{1,2,0:T(4,128)}, u32[]{:S(2)}) %copy-start.9) | copy-done | bytes 5784
  7.2 0.0 copy-start.10
  7.2 0.7 %copy-done.10 = f32[1,360,4]{1,2,0:T(4,128)S(1)} copy-done((f32[1,360,4]{1,2,0:T(4,128)S(1)}, f32[1,360,4]{1,2,0:T(4,128)}, u32[]{:S(2)}) %copy-start.10) | copy-done | bytes 5784
  7.9 44.9 %shard_map.156 = (f32[360,256]{1,0:T(8,128)S(1)}, f32[8,180,128]{2,1,0:T(8,128)S(1)}, f32[9,32,64]{2,1,0:T(8,128)S(1)}, f32[9,16,32]{2,1,0:T(8,128)S(1)}) custom-call(bf16[360,256]{1,0:T(8,128)(2,1)S(1)} %bitcast.22, bf16[8,180,128]{2,1,0:T(8,128)(2,1)S(1)} %get-tuple-element.17.p_ref, s32[8,180]{1,0:T(8,128)S(1)} %copy-done.8, ...), custom_call_target="tpu_custom_call" | custom-call | tf_op jit(solution)/shard_map/pallas_call | solution.py:473
  52.8 1.0 %copy.19 = f32[1,8,180,128]{3,1,2,0:T(8,128)} copy(f32[1,8,180,128]{3,2,1,0:T(8,128)S(1)} %bitcast.19) | data formatting | bytes 1474560
  53.8 0.7 %copy.25 = f32[1,1,360,256]{3,2,1,0:T(8,128)} copy(f32[1,1,360,256]{3,2,1,0:T(8,128)S(1)} %bitcast.20) | data formatting | bytes 737280
  54.6 0.7 %copy.26 = f32[9,32,64]{2,1,0:T(8,128)} copy(f32[9,32,64]{2,1,0:T(8,128)S(1)} %get-tuple-element.24) | data formatting | bytes 147456
  55.2 0.6 %copy.27 = f32[9,16,32]{2,1,0:T(8,128)} copy(f32[9,16,32]{2,1,0:T(8,128)S(1)} %get-tuple-element.25) | data formatting | bytes 36864
Async XLA Ops:
  0.6 1.4 %copy-start.6 = (s32[2,720,4]{1,2,0:T(4,128)S(1)}, s32[2,720,4]{1,2,0:T(4,128)}, u32[]{:S(2)}) copy-start(s32[2,720,4]{1,2,0:T(4,128)} %param.20) | copy-start | bytes 69124
  0.6 1.4 %copy-start.1 = (bf16[9,128,128]{2,1,0:T(8,128)(2,1)S(1)}, bf16[9,128,128]{2,1,0:T(8,128)(2,1)}, u32[]{:S(2)}) copy-start(bf16[9,128,128]{2,1,0:T(8,128)(2,1)} %param.17) | copy-start | bytes 884740
  0.7 1.6 %copy-start = (bf16[9,256,256]{2,1,0:T(8,128)(2,1)S(1)}, bf16[9,256,256]{2,1,0:T(8,128)(2,1)}, u32[]{:S(2)}) copy-start(bf16[9,256,256]{2,1,0:T(8,128)(2,1)} %param.16) | copy-start | bytes 3538948
  0.7 1.6 %copy-start.8 = (s32[8,180]{1,0:T(8,128)S(1)}, s32[8,180]{1,0:T(8,128)}, u32[]{:S(2)}) copy-start(s32[8,180]{1,0:T(8,128)} %wet_ref.1) | copy-start | bytes 17284
  2.2 0.9 %copy-start.2 = (bf16[1,1,360,256]{3,2,1,0:T(8,128)(2,1)S(1)}, bf16[1,1,360,256]{3,2,1,0:T(8,128)(2,1)}, u32[]{:S(2)}) copy-start(bf16[1,1,360,256]{3,2,1,0:T(8,128)(2,1)} %param.13) | copy-start | bytes 552964
  3.2 0.9 %copy-start.3 = (bf16[1,1,360,256]{3,2,1,0:T(8,128)(2,1)S(1)}, bf16[1,1,360,256]{3,2,1,0:T(8,128)(2,1)}, u32[]{:S(2)}) copy-start(bf16[1,1,360,256]{3,2,1,0:T(8,128)(2,1)} %param.24) | copy-start | bytes 552964
  4.1 0.8 %copy-start.4 = (bf16[256,128]{1,0:T(8,128)(2,1)S(1)}, bf16[256,128]{1,0:T(8,128)(2,1)}, u32[]{:S(2)}) copy-start(bf16[256,128]{1,0:T(8,128)(2,1)} %emit_ref.1) | copy-start | bytes 196612
  4.9 0.8 %copy-start.5 = (bf16[128,256]{1,0:T(8,128)(2,1)S(1)}, bf16[128,256]{1,0:T(8,128)(2,1)}, u32[]{:S(2)}) copy-start(bf16[128,256]{1,0:T(8,128)(2,1)} %drive_ref.1) | copy-start | bytes 196612
  5.8 0.7 %copy-start.7 = (f32[2,720,4]{1,2,0:T(4,128)S(1)}, f32[2,720,4]{1,2,0:T(4,128)}, u32[]{:S(2)}) copy-start(f32[2,720,4]{1,2,0:T(4,128)} %param.21) | copy-start | bytes 69124
  6.5 0.7 %copy-start.9 = (s32[1,360,4]{1,2,0:T(4,128)S(1)}, s32[1,360,4]{1,2,0:T(4,128)}, u32[]{:S(2)}) copy-start(s32[1,360,4]{1,2,0:T(4,128)} %param.22) | copy-start | bytes 17284
  7.2 0.7 %copy-start.10 = (f32[1,360,4]{1,2,0:T(4,128)S(1)}, f32[1,360,4]{1,2,0:T(4,128)}, u32[]{:S(2)}) copy-start(f32[1,360,4]{1,2,0:T(4,128)} %param.23) | copy-start | bytes 17284
